TPU v7x, 128 devices: a whole 4x4x4 slice. The times are simulated.
128 devices in a mesh: tiles: 16 (over x, z), cols: 8 (over y, core).
Axes of the slice: x: 4, y: 4, z: 4, core: 2. Of those that a mesh axis runs over, the one named last changes fastest.
Arguments:
- object_field: float32 [2, 2, 4096, 2048], P(None, None, 'tiles', 'cols')
- probe: float32 [2, 4, 128, 128], replicated, may hold values from -3 to 3
- row_offsets: int32 [16, 8, 8], P('tiles', 'cols'), may hold values from 0 to 255, as said below
- col_offsets: int32 [16, 8, 8], P('tiles', 'cols'), may hold values from 0 to 255, as said below
- counts: int32 [16, 8], P('tiles', 'cols'), may hold values from 1 to 8, as said below
- measured: float32 [16, 8, 8, 128, 128], P('tiles', 'cols'), may hold values from 0.25 to 2.5
Outputs:
- new_object: float32 [2, 2, 4096, 2048], P(None, None, 'tiles', 'cols')
- new_probe: float32 [2, 4, 128, 128], replicated
Inputs may be any that keep to these rules, and one draw needn't show every extreme that they name: `row_offsets`: A patch never leaves the object region: on the last row of tiles the offset is at most 128; elsewhere it may reach into the tile below. `col_offsets`: A patch never leaves the object region: on the last column of tiles the offset is at most 128; elsewhere it may reach into the tile to the right. `counts`: slots from a device's count on are unused; some device has 8 live positions.
All inputs are finite; a program needn't handle non-finite values.
Results may differ from a plain program's by a relative error of at most 0.0001.
Values sent between devices are 32-bit elements; how exact they have to be, the bound alone decides.
A program may use at most 128 MiB of HBM per device.

v0:
```python
import math

import jax
import jax.numpy as jnp
from jax import lax
from jax.sharding import PartitionSpec as P

ITERS = 2


step_object = 0.25
exact = lax.Precision.HIGHEST


def from_behind(block, axis, distance):
    devices = range(lax.axis_size(axis))
    route = [(i - distance, i) for i in devices if i - distance in devices]
    return lax.ppermute(block, axis, route)


def fresnel_kernel(size):
    index_line = jnp.arange(size, dtype=jnp.int32)
    freq = jnp.where(index_line < size // 2, index_line, index_line - size)
    square = freq * freq
    phase_index = (square[:, None] + square[None, :]) % (4 * size)
    angle = -2.0 * math.pi / (4 * size) * phase_index.astype(jnp.float32)
    return jnp.stack([jnp.cos(angle), jnp.sin(angle)])


def dft_tables(size):
    index_line = jnp.arange(size, dtype=jnp.int32)
    phase_index = index_line[:, None] * index_line[None, :] % size
    angle = 2.0 * math.pi / size * phase_index.astype(jnp.float32)
    scale = 1.0 / math.sqrt(size)
    return (jnp.cos(angle) * scale, -jnp.sin(angle) * scale)


def times(first, second):
    return jnp.stack(
        [first[0] * second[0] - first[1] * second[1], first[0] * second[1] + first[1] * second[0]]
    )


def conjugate(value):
    return jnp.stack([value[0], -value[1]])


def transform(field, tables, sign):
    real_table = tables[0]
    imag_table = tables[1] * sign
    left_real = jnp.einsum("ab,zmbc->zmac", real_table, field, precision=exact)
    left_imag = jnp.einsum("ab,zmbc->zmac", imag_table, field, precision=exact)
    middle = jnp.stack([left_real[0] - left_imag[1], left_real[1] + left_imag[0]])
    right_real = jnp.einsum("zmab,bc->zmac", middle, real_table, precision=exact)
    right_imag = jnp.einsum("zmab,bc->zmac", middle, imag_table, precision=exact)
    return jnp.stack([right_real[0] - right_imag[1], right_real[1] + right_imag[0]])


def position_grads(patch, data, beam, kernel, tables):
    slices = patch.shape[1]
    psi = times(beam, patch[:, 0][:, None])
    s = 1
    spread = transform(times(transform(psi, tables, 1.0), kernel[:, None]), tables, -1.0)
    carried = [spread]
    psi = times(spread, patch[:, s][:, None])
    far = transform(psi, tables, 1.0)
    intensity_pattern = jnp.sum(far[0] * far[0] + far[1] * far[1], axis=0)
    back = transform(far * (intensity_pattern - data)[None, None], tables, -1.0)
    kernel_conj = conjugate(kernel)[:, None]
    grads = [patch[:, 0]] * slices
    s = 1
    grads[s] = jnp.sum(times(conjugate(carried[s - 1]), back), axis=1)
    back = times(conjugate(patch[:, s][:, None]), back)
    back = transform(times(transform(back, tables, 1.0), kernel_conj), tables, -1.0)
    grads[0] = jnp.sum(times(conjugate(beam), back), axis=1)
    probe_term = times(conjugate(patch[:, 0][:, None]), back)
    return (jnp.stack(grads, axis=1), probe_term)


def widen(field, size):
    below = from_behind(field[:, :, :size, :], "tiles", -1)
    side = from_behind(field[:, :, :, :size], "cols", -1)
    moved = from_behind(field[:, :, :size, :size], "cols", -1)
    corner = from_behind(moved, "tiles", -1)
    upper = jnp.concatenate([field, side], axis=3)
    lower = jnp.concatenate([below, corner], axis=3)
    return jnp.concatenate([upper, lower], axis=2)


def narrow(grad_ext, tile_rows, tile_cols, size):
    own = grad_ext[:, :, :tile_rows, :tile_cols]
    below = from_behind(grad_ext[:, :, tile_rows:, :tile_cols], "tiles", 1)
    side = from_behind(grad_ext[:, :, :tile_rows, tile_cols:], "cols", 1)
    moved = from_behind(grad_ext[:, :, tile_rows:, tile_cols:], "cols", 1)
    corner = from_behind(moved, "tiles", 1)
    own = own.at[:, :, :size, :].add(below)
    own = own.at[:, :, :, :size].add(side)
    own = own.at[:, :, :size, :size].add(corner)
    return own


def gradients(extended, beam, rows, cols, count, data_all, kernel, tables):
    slices = extended.shape[1]
    size = beam.shape[-1]
    zero = jnp.zeros((), jnp.int32)

    def window(row_index, column_index):
        return lax.dynamic_slice(
            extended, (zero, zero, row_index, column_index), (2, slices, size, size)
        )

    def add_patch(total, grad_patch, row_index, column_index):
        start = (zero, zero, row_index, column_index)
        current = lax.dynamic_slice(total, start, (2, slices, size, size))
        return lax.dynamic_update_slice(total, current + grad_patch, start)

    def visit(slot, carry):
        total, beam_sum = carry
        row_index = rows[slot]
        column_index = cols[slot]
        grad_patch, probe_term = position_grads(
            window(row_index, column_index), data_all[slot], beam, kernel, tables
        )
        return (add_patch(total, grad_patch, row_index, column_index), beam_sum + probe_term)

    start = (jnp.zeros_like(extended), jnp.zeros_like(beam))
    grad_ext, grad_beam = lax.fori_loop(0, count, visit, start)
    return (grad_ext, grad_beam)


def local(object_field, probe, row_offsets, col_offsets, counts, measured):
    size = probe.shape[-1]
    tile_rows = object_field.shape[2]
    tile_cols = object_field.shape[3]
    capacity = row_offsets.shape[-1]
    step_probe = 1.0 / (lax.axis_size("tiles") * lax.axis_size("cols") * capacity)
    kernel = fresnel_kernel(size)
    tables = dft_tables(size)
    rows = row_offsets.reshape(capacity)
    cols = col_offsets.reshape(capacity)
    count_arr = counts.reshape(1)
    count = count_arr[0]
    data_all = measured.reshape(capacity, size, size)
    field = object_field
    beam = probe
    for sweep in range(ITERS):
        extended = widen(field, size)
        grad_ext, grad_beam = gradients(extended, beam, rows, cols, count, data_all, kernel, tables)
        grad_beam = lax.psum(grad_beam, ("tiles", "cols"))
        grad_tile = narrow(grad_ext, tile_rows, tile_cols, size)
        field = field - step_object * grad_tile
        beam = beam - step_probe * grad_beam
    return (field, beam)


def solution(mesh):
    in_specs = (
        P(None, None, "tiles", "cols"),
        P(),
        P("tiles", "cols", None),
        P("tiles", "cols", None),
        P("tiles", "cols"),
        P("tiles", "cols", None, None, None),
    )
    out_specs = (P(None, None, "tiles", "cols"), P())
    return jax.shard_map(local, mesh=mesh, in_specs=in_specs, out_specs=out_specs, check_vma=False)
```

profile of v0, /device:TPU:1, one launch (start us, length us, event | category | flops | bytes accessed | tf_op | source)
XLA Modules:
  0.0 1063.6 jit_solution(3145885099176892727)
XLA Ops:
  9.7 3.3 collective-permute-start
  15.1 1.9 collective-permute-start.2
  17.4 7.1 collective-permute-done.2
  26.1 4.0 collective-permute-done.1
  30.0 5.0 collective-permute-done.3
  35.0 2.6 maximum_maximum_fusion
  39.3 44.7 %while.42 = (s32[]{:T(128)}, f32[2,2,384,384]{3,2,1,0:T(8,128)}, f32[2,4,128,128]{2,3,1,0:T(8,128)S(1)}, s32[]{:T(128)}, s32[8]{0:T(128)S(1)}, /*index=5*/s32[8]...) while((s32[]{:T(128)}, f32[2,2,384,384]{3,2,1,0:T(8,128)}, ...), condition=%wide.region_4.5_spmd.clone.clone.clone, body=%wide.region_0.4_spmd.clone.clone.clone.sunk | while | flops 4847517696 | bytes 59639200 | solution.py:127
  78.6 4.4 dynamic_update_slice.20
  85.2 3.7 collective-permute-start.4
  89.9 134.5 %collective-permute-start.6 = (f32[2,2,128,128]{3,2,1,0:T(8,128)S(1)}, f32[2,2,128,128]{3,2,1,0:T(8,128)S(1)}, u32[]{:S(2)}, u32[]{:S(2)}) collective-permute-start(f32[2,2,128,128]{3,2,1,0:T(8,128)S(1)} %slice.976), channel_id=1, source_target_pairs={{0,1},{1,2},{2,3},{3,4},{4,5},{5,6},{6,7},{8,9},{9,10},{10,11},{11... | collective-permute-start | bytes 786440 | tf_op jit(solution)/shard_map/ppermute | solution.py:18
  225.5 131.1 %collective-permute-start.5 = (f32[2,2,256,128]{3,2,1,0:T(8,128)S(1)}, f32[2,2,256,128]{3,2,1,0:T(8,128)S(1)}, u32[]{:S(2)}, u32[]{:S(2)}) collective-permute-start(f32[2,2,256,128]{3,2,1,0:T(8,128)S(1)} %slice.974), channel_id=1, source_target_pairs={{0,1},{1,2},{2,3},{3,4},{4,5},{5,6},{6,7},{8,9},{9,10},{10,11},{11... | collective-permute-start | bytes 1572872 | tf_op jit(solution)/shard_map/ppermute | solution.py:18
  358.2 4.5 collective-permute-done.5
  363.1 2.1 collective-permute-start.10
  373.1 184.6 %all-reduce.3.cloned.1.call-done = f32[2,4,128,128]{3,2,1,0:T(8,128)} async-done(((f32[2,4,128,128]{3,2,1,0:T(8,128)}), f32[2,4,128,128]{3,2,1,0:T(8,128)}) %all-reduce.3.cloned.1.call-update) | async-done | bytes 524304 | tf_op jit(solution)/shard_map/psum | solution.py:149
  559.2 2.8 maximum_maximum_fusion.1
  563.6 43.2 %while.43 = (s32[]{:T(128)}, f32[2,2,384,384]{3,2,1,0:T(8,128)}, f32[2,4,128,128]{2,3,1,0:T(8,128)S(1)}, s32[]{:T(128)}, s32[8]{0:T(128)S(1)}, /*index=5*/s32[8]...) while((s32[]{:T(128)}, f32[2,2,384,384]{3,2,1,0:T(8,128)}, ...), condition=%wide.region_10.11_spmd.clone.clone.clone, body=%wide.region_6.0_spmd.clone.clone.clone.sunk | while | flops 4847517696 | bytes 59639156 | solution.py:127
  601.6 4.4 dynamic_update_slice.21
  609.8 3.3 collective-permute-start.12
  614.8 128.2 %collective-permute-start.13 = (f32[2,2,256,128]{3,2,1,0:T(8,128)}, f32[2,2,256,128]{3,2,1,0:T(8,128)}, u32[]{:S(2)}, u32[]{:S(2)}) collective-permute-start(f32[2,2,256,128]{3,2,1,0:T(8,128)} %slice.985), channel_id=1, source_target_pairs={{0,1},{1,2},{2,3},{3,4},{4,5},{5,6},{6,7},{8,9},{9,10},{10,11},{11... | collective-permute-start | bytes 1572872 | tf_op jit(solution)/shard_map/ppermute | solution.py:18
  743.1 128.2 %collective-permute-start.14 = (f32[2,2,128,128]{3,2,1,0:T(8,128)}, f32[2,2,128,128]{3,2,1,0:T(8,128)}, u32[]{:S(2)}, u32[]{:S(2)}) collective-permute-start(f32[2,2,128,128]{3,2,1,0:T(8,128)} %slice.987), channel_id=1, source_target_pairs={{0,1},{1,2},{2,3},{3,4},{4,5},{5,6},{6,7},{8,9},{9,10},{10,11},{11... | collective-permute-start | bytes 786440 | tf_op jit(solution)/shard_map/ppermute | solution.py:18
  871.2 173.8 %all-reduce.5.cloned.1.call-done = f32[2,4,128,128]{3,2,1,0:T(8,128)} async-done(((f32[2,4,128,128]{3,2,1,0:T(8,128)}), f32[2,4,128,128]{3,2,1,0:T(8,128)}) %all-reduce.5.cloned.1.call-update) | async-done | bytes 524304 | tf_op jit(solution)/shard_map/psum | solution.py:149
  1045.1 2.0 multiply_subtract_fusion.18
  1047.1 2.7 collective-permute-start.15
  1052.1 3.1 collective-permute-done.15
  (197 shorter events, 99.8 us)
Async XLA Ops:
  7.2 18.7 %copy-start.7 = (f32[2,4,128,128]{3,2,1,0:T(8,128)S(1)}, f32[2,4,128,128]{3,2,1,0:T(8,128)}, u32[]{:S(2)}) copy-start(f32[2,4,128,128]{3,2,1,0:T(8,128)} %param.23) | copy-start | bytes 1572868
  7.2 550.5 %all-reduce.3.cloned.1.call-start = ((), (), s32[]{:S(2)}) async-start(), calls=%async_computation | async-start | bytes 1048576 | tf_op jit(solution)/shard_map/psum | solution.py:149
  9.7 16.4 %collective-permute-start = (f32[2,2,256,128]{2,3,1,0:T(8,128)}, f32[2,2,256,128]{2,3,1,0:T(8,128)S(1)}, u32[]{:S(2)}, u32[]{:S(2)}) collective-permute-start(f32[2,2,256,128]{2,3,1,0:T(8,128)} %slice.1420), channel_id=1, source_target_pairs={{1,0},{2,1},{3,2},{4,3},{5,4},{6,5},{7,6},{9,8},{10,9},{11,10},{12... | collective-permute-start | bytes 1572872 | tf_op jit(solution)/shard_map/ppermute | solution.py:18
  13.8 16.2 %collective-permute-start.1 = (f32[2,2,128,256]{2,3,1,0:T(8,128)}, f32[2,2,128,256]{2,3,1,0:T(8,128)}, u32[]{:S(2)}, u32[]{:S(2)}) collective-permute-start(f32[2,2,128,256]{2,3,1,0:T(8,128)} %slice.1421), channel_id=1, source_target_pairs={{8,0},{16,8},{24,16},{32,24},{40,32},{48,40},{56,48},{64,56},{72,6... | collective-permute-start | bytes 1572872 | tf_op jit(solution)/shard_map/ppermute | solution.py:18
  15.1 9.4 collective-permute-start.2
  24.5 10.5 collective-permute-start.3
  84.0 272.6 %copy-start.3 = (f32[2,2,384,384]{3,2,1,0:T(8,128)S(1)}, f32[2,2,384,384]{3,2,1,0:T(8,128)}, u32[]{:S(2)}) copy-start(f32[2,2,384,384]{3,2,1,0:T(8,128)} %get-tuple-element.632) | copy-start | bytes 7077892
  85.2 272.9 %collective-permute-start.4 = (f32[2,2,128,256]{3,2,1,0:T(8,128)S(1)}, f32[2,2,128,256]{3,2,1,0:T(8,128)S(1)}, u32[]{:S(2)}, u32[]{:S(2)}) collective-permute-start(f32[2,2,128,256]{3,2,1,0:T(8,128)S(1)} %slice.972), channel_id=1, source_target_pairs={{0,8},{8,16},{16,24},{24,32},{32,40},{40,48},{48,56},{56,64},{64,7... | collective-permute-start | bytes 1572872 | tf_op jit(solution)/shard_map/ppermute | solution.py:18
  89.9 266.8 %collective-permute-start.6 = (f32[2,2,128,128]{3,2,1,0:T(8,128)S(1)}, f32[2,2,128,128]{3,2,1,0:T(8,128)S(1)}, u32[]{:S(2)}, u32[]{:S(2)}) collective-permute-start(f32[2,2,128,128]{3,2,1,0:T(8,128)S(1)} %slice.976), channel_id=1, source_target_pairs={{0,1},{1,2},{2,3},{3,4},{4,5},{5,6},{6,7},{8,9},{9,10},{10,11},{11... | collective-permute-start | bytes 786440 | tf_op jit(solution)/shard_map/ppermute | solution.py:18
  225.5 137.2 %collective-permute-start.5 = (f32[2,2,256,128]{3,2,1,0:T(8,128)S(1)}, f32[2,2,256,128]{3,2,1,0:T(8,128)S(1)}, u32[]{:S(2)}, u32[]{:S(2)}) collective-permute-start(f32[2,2,256,128]{3,2,1,0:T(8,128)S(1)} %slice.974), channel_id=1, source_target_pairs={{0,1},{1,2},{2,3},{3,4},{4,5},{5,6},{6,7},{8,9},{9,10},{10,11},{11... | collective-permute-start | bytes 1572872 | tf_op jit(solution)/shard_map/ppermute | solution.py:18
  356.7 6.2 collective-permute-start.7
  363.0 196.2 %copy-start = (f32[2,2,256,256]{3,2,1,0:T(8,128)}, f32[2,2,256,256]{3,2,1,0:T(8,128)S(1)}, u32[]{:S(2)}) copy-start(f32[2,2,256,256]{3,2,1,0:T(8,128)S(1)} %multiply_subtract_fusion.17) | copy-start | bytes 3145732
  363.1 194.6 %copy-start.8 = (f32[2,4,128,128]{3,2,1,0:T(8,128)S(1)}, f32[2,4,128,128]{3,2,1,0:T(8,128)}, u32[]{:S(2)}) copy-start(f32[2,4,128,128]{3,2,1,0:T(8,128)} %param.23) | copy-start | bytes 1572868
  363.1 8.7 collective-permute-start.10
  366.2 678.9 %all-reduce.5.cloned.1.call-start = ((), (), s32[]{:S(2)}) async-start(), calls=%async_computation.1 | async-start | bytes 1048576 | tf_op jit(solution)/shard_map/psum | solution.py:149
  367.9 191.3 %collective-permute-start.8 = (f32[2,2,256,128]{3,2,1,0:T(8,128)}, f32[2,2,256,128]{3,2,1,0:T(8,128)}, u32[]{:S(2)}, u32[]{:S(2)}) collective-permute-start(f32[2,2,256,128]{3,2,1,0:T(8,128)} %slice.1426), channel_id=1, source_target_pairs={{1,0},{2,1},{3,2},{4,3},{5,4},{6,5},{7,6},{9,8},{10,9},{11,10},{12... | collective-permute-start | bytes 1572872 | tf_op jit(solution)/shard_map/ppermute | solution.py:18
  369.8 189.4 %collective-permute-start.9 = (f32[2,2,128,256]{3,2,1,0:T(8,128)}, f32[2,2,128,256]{3,2,1,0:T(8,128)}, u32[]{:S(2)}, u32[]{:S(2)}) collective-permute-start(f32[2,2,128,256]{3,2,1,0:T(8,128)} %slice.1427), channel_id=1, source_target_pairs={{8,0},{16,8},{24,16},{32,24},{40,32},{48,40},{56,48},{64,56},{72,6... | collective-permute-start | bytes 1572872 | tf_op jit(solution)/shard_map/ppermute | solution.py:18
  371.8 187.4 %collective-permute-start.11 = (f32[2,2,128,128]{3,2,1,0:T(8,128)}, f32[2,2,128,128]{3,2,1,0:T(8,128)S(1)}, u32[]{:S(2)}, u32[]{:S(2)}) collective-permute-start(f32[2,2,128,128]{3,2,1,0:T(8,128)} %collective-permute-done.10), channel_id=1, source_target_pairs={{8,0},{16,8},{24,16},{32,24},{40,32},{48,40},{56,48},{64,56},{72,6... | collective-permute-start | bytes 786440 | tf_op jit(solution)/shard_map/ppermute | solution.py:18
  606.9 6.3 copy-start.2
  609.8 440.0 %collective-permute-start.12 = (f32[2,2,128,256]{3,2,1,0:T(8,128)}, f32[2,2,128,256]{3,2,1,0:T(8,128)}, u32[]{:S(2)}, u32[]{:S(2)}) collective-permute-start(f32[2,2,128,256]{3,2,1,0:T(8,128)} %slice.983), channel_id=1, source_target_pairs={{0,8},{8,16},{16,24},{24,32},{32,40},{40,48},{48,56},{56,64},{64,7... | collective-permute-start | bytes 1572872 | tf_op jit(solution)/shard_map/ppermute | solution.py:18
  614.8 436.1 %collective-permute-start.13 = (f32[2,2,256,128]{3,2,1,0:T(8,128)}, f32[2,2,256,128]{3,2,1,0:T(8,128)}, u32[]{:S(2)}, u32[]{:S(2)}) collective-permute-start(f32[2,2,256,128]{3,2,1,0:T(8,128)} %slice.985), channel_id=1, source_target_pairs={{0,1},{1,2},{2,3},{3,4},{4,5},{5,6},{6,7},{8,9},{9,10},{10,11},{11... | collective-permute-start | bytes 1572872 | tf_op jit(solution)/shard_map/ppermute | solution.py:18
  743.1 304.1 %collective-permute-start.14 = (f32[2,2,128,128]{3,2,1,0:T(8,128)}, f32[2,2,128,128]{3,2,1,0:T(8,128)}, u32[]{:S(2)}, u32[]{:S(2)}) collective-permute-start(f32[2,2,128,128]{3,2,1,0:T(8,128)} %slice.987), channel_id=1, source_target_pairs={{0,1},{1,2},{2,3},{3,4},{4,5},{5,6},{6,7},{8,9},{9,10},{10,11},{11... | collective-permute-start | bytes 786440 | tf_op jit(solution)/shard_map/ppermute | solution.py:18
  1047.1 8.2 copy-start.1
  1047.1 8.2 collective-permute-start.15
  (5 other events, 17.8 us)
Sparse Core Ops, SparseCore 0:
  366.3 191.3 all-reduce.2
  608.1 436.9 all-reduce.4
where the time goes:
time: 1070 us; the launch traced here: 1060 us
  starting transfers between devices  547 us (51%)
  waiting for transfers between devices  383 us (36%)
  matrix products  52 us (5%)
  local copies, waits for them, and re-layouts  35 us (3%)
  other arithmetic  19.7 us (2%)
  between operations  14.8 us (1%)
  loops' own time  11.8 us (1%)
    ppermute x16, starting transfers between devices, from_behind(): return lax.ppermute(block, axis, route)  547 us
    psum x2, waiting for transfers between devices, local(): grad_beam = lax.psum(grad_beam, ('tiles', 'cols'))  358 us
    ppermute x16, waiting for transfers between devices, from_behind(): return lax.ppermute(block, axis, route)  24.3 us
  transfers between devices with their start and end apart: 18, of which 8 were waited for; matrix products, arithmetic and copies ran while one was open for 1% of the time, Pallas kernels for 0%

commit v1 on v0

v1 whole, which is shorter than its diff:
```python
import functools
import math

import jax
import jax.numpy as jnp
import ml_dtypes
import numpy as np
from jax import lax
from jax.experimental import pallas as pl
from jax.experimental.pallas import tpu as pltpu
from jax.sharding import PartitionSpec as P

ITERS = 2
STEP_OBJECT = 0.25
f32, bf16 = jnp.float32, jnp.bfloat16
MESH = pl.DeviceIdType.MESH
VMEM_LIMIT = 56 * 2**20

A_PLUS, A_MINUS, F_PLUS, F_MINUS = 0, 2, 4, 6


def split_table(table):
    high = table.astype(np.float32).astype(ml_dtypes.bfloat16)
    low = (table - high.astype(np.float64)).astype(np.float32).astype(ml_dtypes.bfloat16)
    return [high, low]


def transform_tables(size):
    line = np.arange(size)
    dft = np.exp(-2j * np.pi * (np.outer(line, line) % size) / size) / math.sqrt(size)
    freq = np.where(line < size // 2, line, line - size)
    chirp = np.exp(-2j * np.pi * ((freq * freq) % (4 * size)) / (4 * size))
    propagator = np.conj(dft) @ (chirp[:, None] * dft)
    parts = []
    for matrix in (propagator, dft):
        real, imag = matrix.real, matrix.imag
        plus = np.block([[real, imag], [-imag, real]])
        parts += split_table(plus) + split_table(plus.T)
    return np.stack(parts)


def split(value):
    high = value.astype(bf16)
    return high, (value - high.astype(f32)).astype(bf16)


def product(first, second):
    dot = functools.partial(jnp.dot, preferred_element_type=f32)
    return dot(first[0], second[0]) + (dot(first[1], second[0]) + dot(first[0], second[1]))


def two_sided(fields, table, left, right):
    n = fields[0][0].shape[0]
    modes = range(len(fields))
    stacked = [jnp.concatenate(field, axis=0) for field in fields]
    middle = product((table[left], table[left + 1]), split(jnp.concatenate(stacked, axis=1)))
    columns = [middle[:, n * m : n * m + n] for m in modes]
    beside = [jnp.concatenate([c[:n], c[n:]], axis=1) for c in columns]
    result = product(split(jnp.concatenate(beside, axis=0)), (table[right], table[right + 1]))
    rows = [result[n * m : n * m + n] for m in modes]
    return [(row[:, :n], row[:, n:]) for row in rows]


def times(a, b):
    return (a[0] * b[0] - a[1] * b[1], a[0] * b[1] + a[1] * b[0])


def conj_times(a, b):
    return (a[0] * b[0] + a[1] * b[1], a[0] * b[1] - a[1] * b[0])


def total(terms):
    real, imag = terms[0]
    for term in terms[1:]:
        real, imag = real + term[0], imag + term[1]
    return real, imag


GROUP = 4


def gradient_kernel(rows, cols, counts, extended, probe, measured, table, grad, grad_probe):
    n = probe.shape[-1]
    modes = range(probe.shape[1])
    grad[...] = jnp.zeros_like(grad)
    grad_probe[...] = jnp.zeros_like(grad_probe)
    lane = lax.broadcasted_iota(jnp.int32, (n, n), 1)
    count = counts[0]

    def visit(step, carry):
        beams = [(probe[0, m], probe[1, m]) for m in modes]
        slots = []
        for k in range(GROUP):
            slot = step * GROUP + k
            live = slot < count
            row = jnp.where(live, rows[slot], 0)
            col = jnp.where(live, cols[slot], 0)
            block = lax.shift_right_logical(col, 7)
            slots.append((slot, jnp.where(live, 1.0, 0.0).astype(f32), row, block, col - block * n))

        def window(plane, slot):
            _, _, row, block, shift = slot
            back = jnp.bitwise_and(n - shift, n - 1)
            near = pltpu.roll(extended[plane, block, pl.ds(row, n), :], back, 1)
            far = pltpu.roll(extended[plane, block + 1, pl.ds(row, n), :], back, 1)
            return jnp.where(lane < n - shift, near, far)

        first = [(window(0, s), window(2, s)) for s in slots]
        spread = [two_sided([times(b, o) for b in beams], table, A_MINUS, A_PLUS) for o in first]
        second = [(window(1, s), window(3, s)) for s in slots]
        far = [
            two_sided([times(o, x) for x in fields], table, F_MINUS, F_PLUS)
            for o, fields in zip(second, spread)
        ]
        residual = []
        for slot, fields in zip(slots, far):
            intensity = sum(y[0] * y[0] + y[1] * y[1] for y in fields)
            residual.append((intensity - measured[slot[0]]) * slot[1])
        back = [
            two_sided([(r * y[0], r * y[1]) for y in fields], table, F_PLUS, F_MINUS)
            for r, fields in zip(residual, far)
        ]
        grad_second = [
            total([conj_times(x, g) for x, g in zip(fields, backs)])
            for fields, backs in zip(spread, back)
        ]
        back = [
            two_sided([conj_times(o, g) for g in backs], table, A_PLUS, A_MINUS)
            for o, backs in zip(second, back)
        ]
        grad_first = [total([conj_times(b, g) for b, g in zip(beams, backs)]) for backs in back]
        for m in modes:
            real, imag = total([conj_times(o, backs[m]) for o, backs in zip(first, back)])
            grad_probe[0, m] += real
            grad_probe[1, m] += imag
        for (_, _, row, block, shift), g0, g1 in zip(slots, grad_first, grad_second):
            kept = lane >= shift
            for plane, value in enumerate((g0[0], g1[0], g0[1], g1[1])):
                moved = pltpu.roll(value, shift, 1)
                grad[plane, block, pl.ds(row, n), :] += jnp.where(kept, moved, 0.0)
                grad[plane, block + 1, pl.ds(row, n), :] += jnp.where(kept, 0.0, moved)
        return carry

    lax.fori_loop(0, (count + GROUP - 1) // GROUP, visit, 0)


SMEM_SPEC = pl.BlockSpec(memory_space=pltpu.SMEM)
VMEM_SPEC = pl.BlockSpec(memory_space=pltpu.VMEM)
ANY_SPEC = pl.BlockSpec(memory_space=pl.ANY)


def gradients(rows, cols, counts, extended, probe, measured, table):
    slots = rows.shape[0]
    work = slots * probe.shape[1] * 8 * 3 * 2 * 256 * 256 * 128
    return pl.pallas_call(
        gradient_kernel,
        out_shape=[
            jax.ShapeDtypeStruct(extended.shape, f32),
            jax.ShapeDtypeStruct(probe.shape, f32),
        ],
        in_specs=[SMEM_SPEC] * 3 + [VMEM_SPEC] * 4,
        out_specs=[VMEM_SPEC] * 2,
        compiler_params=pltpu.CompilerParams(vmem_limit_bytes=VMEM_LIMIT),
        cost_estimate=pl.CostEstimate(flops=work, bytes_accessed=8 * 2**20, transcendentals=0),
        name="gradients",
    )(rows, cols, counts, extended, probe, measured, table)


class Place:
    def __init__(self, tiles, cols):
        self.tiles, self.cols = tiles, cols
        self.t, self.c = lax.axis_index("tiles"), lax.axis_index("cols")

    def at(self, down, right):
        return (
            lax.rem(self.t + (down + self.tiles), self.tiles),
            lax.rem(self.c + (right + self.cols), self.cols),
        )


def greet(devices):
    barrier = pltpu.get_barrier_semaphore()
    for device in devices:
        pl.semaphore_signal(barrier, inc=1, device_id=device, device_id_type=MESH)
    pl.semaphore_wait(barrier, len(devices))


class Copies:
    def __init__(self, send, recv):
        self.send, self.recv, self.used, self.started = send, recv, 0, []

    def start(self, source, target, device):
        k = self.used
        self.used += 1
        copy = pltpu.make_async_remote_copy(
            src_ref=source,
            dst_ref=target,
            send_sem=self.send.at[k],
            recv_sem=self.recv.at[k],
            device_id=device,
            device_id_type=MESH,
        )
        copy.start()
        self.started.append(copy)
        return copy

    def finish(self):
        for copy in self.started:
            copy.wait_send()


def widen_kernel(tiles, cols, size, field, extended, local_sem, send, recv):
    planes, height, width = field.shape
    blocks = width // size
    place = Place(tiles, cols)
    own = []
    for j in range(blocks):
        copy = pltpu.make_async_copy(
            field.at[:, :, pl.ds(j * size, size)],
            extended.at[:, j, pl.ds(0, height), :],
            local_sem.at[j],
        )
        copy.start()
        own.append(copy)
    greet([place.at(d, r) for d, r in ((-1, -1), (-1, 0), (0, -1), (1, 1), (1, 0), (0, 1))])
    copies = Copies(send, recv)
    up, left, corner = place.at(-1, 0), place.at(0, -1), place.at(-1, -1)
    top = pl.ds(0, size)
    below = pl.ds(height, size)
    for j in range(blocks):
        copies.start(field.at[:, top, pl.ds(j * size, size)], extended.at[:, j, below, :], up)
    copies.start(field.at[:, top, pl.ds(0, size)], extended.at[:, blocks, below, :], corner)
    copies.start(
        field.at[:, :, pl.ds(0, size)], extended.at[:, blocks, pl.ds(0, height), :], left
    )
    for copy in own:
        copy.wait()
    for copy in copies.started:
        copy.wait_recv()
    copies.finish()


def widen(field, size, tiles, cols):
    planes, height, width = field.shape
    blocks = width // size
    return pl.pallas_call(
        functools.partial(widen_kernel, tiles, cols, size),
        out_shape=jax.ShapeDtypeStruct((planes, blocks + 1, height + size, size), f32),
        in_specs=[ANY_SPEC],
        out_specs=VMEM_SPEC,
        scratch_shapes=[
            pltpu.SemaphoreType.DMA((blocks,)),
            pltpu.SemaphoreType.DMA((blocks + 2,)),
            pltpu.SemaphoreType.DMA((blocks + 2,)),
        ],
        compiler_params=pltpu.CompilerParams(
            collective_id=0, has_side_effects=True, vmem_limit_bytes=VMEM_LIMIT
        ),
        name="widen",
    )(field)


class ProbeSum:
    def __init__(self, place, copies, grad, pair, pieces, column, halves):
        self.place, self.copies = place, copies
        self.grad, self.pair, self.pieces, self.column, self.halves = grad, pair, pieces, column, halves
        self.half = grad.shape[0] // 2
        self.piece = self.half // place.tiles
        self.core = lax.rem(place.c, 2)
        self.partner = (place.t, place.c + 1 - 2 * self.core)
        self.mine = pl.ds(self.core * self.half, self.half)
        self.others = pl.ds((1 - self.core) * self.half, self.half)

    def scatter_pair(self):
        self.step = self.copies.start(self.grad.at[self.others], self.pair, self.partner)

    def scatter_tiles(self):
        self.step.wait_recv()
        self.grad[self.mine] += self.pair[...]
        place, piece = self.place, self.piece
        self.steps = []
        for k in range(1, place.tiles):
            peer = lax.rem(place.t + k, place.tiles)
            source = self.grad.at[pl.ds(self.core * self.half + peer * piece, piece)]
            self.steps.append(
                self.copies.start(source, self.pieces.at[k - 1], (peer, place.c))
            )

    def sum_column(self):
        place, piece = self.place, self.piece
        value = self.grad[pl.ds(self.core * self.half + place.t * piece, piece)]
        for k, step in enumerate(self.steps):
            step.wait_recv()
            value += self.pieces[k]
        chips = place.cols // 2
        chip = place.c // 2
        self.column[chip] = value
        self.steps = []
        for k in range(1, chips):
            peer = (place.t, lax.rem(place.c + 2 * k, place.cols))
            self.steps.append(
                self.copies.start(self.column.at[chip], self.column.at[chip], peer)
            )

    def gather_tiles(self):
        for step in self.steps:
            step.wait_recv()
        place, piece = self.place, self.piece
        value = self.column[0]
        for k in range(1, place.cols // 2):
            value += self.column[k]
        own = pl.ds(self.core * self.half + place.t * piece, piece)
        self.halves[own] = value
        self.steps = []
        for k in range(1, place.tiles):
            peer = lax.rem(place.t + k, place.tiles)
            self.steps.append(
                self.copies.start(self.halves.at[own], self.halves.at[own], (peer, place.c))
            )

    def gather_pair(self):
        for step in self.steps:
            step.wait_recv()
        self.step = self.copies.start(
            self.halves.at[self.mine], self.halves.at[self.mine], self.partner
        )

    def result(self):
        self.step.wait_recv()
        return self.halves[...]

    @staticmethod
    def copies_needed(tiles, cols):
        return 2 * tiles + cols // 2 - 1

    @staticmethod
    def scratch(rows, lanes, tiles, cols):
        half = rows // 2
        piece = half // tiles
        return [
            pltpu.VMEM((half, lanes), f32),
            pltpu.VMEM((tiles - 1, piece, lanes), f32),
            pltpu.VMEM((cols // 2, piece, lanes), f32),
            pltpu.VMEM((rows, lanes), f32),
        ]


def met(place):
    devices = [place.at(k, 0) for k in range(1, place.tiles)]
    return devices + [
        place.at(0, k) for k in range(1, place.cols) if k % 2 == 0 or k in (1, place.cols - 1)
    ]


def exchange_kernel(
    tiles,
    cols,
    grad,
    extended,
    grad_probe,
    probe,
    new_extended,
    new_probe,
    from_left,
    from_right,
    from_up,
    from_down,
    from_corner,
    pair,
    pieces,
    column,
    halves,
    send,
    recv,
):
    planes, count, tall, size = grad.shape
    last = count - 1
    height = tall - size
    top, middle, below = pl.ds(0, size), pl.ds(size, height - size), pl.ds(height, size)
    place = Place(tiles, cols)
    greet(met(place))
    copies = Copies(send, recv)
    up, down, left, right = place.at(-1, 0), place.at(1, 0), place.at(0, -1), place.at(0, 1)
    reduce = ProbeSum(place, copies, grad_probe, pair, pieces, column, halves)
    every = range(planes)
    reduce.scatter_pair()
    sides = [copies.start(grad.at[p, last], from_left.at[p], right) for p in every]
    ups, downs = {}, {}
    for j in list(range(1, last)) + [0]:
        for p in every:
            if j == 0:
                sides[p].wait_recv()
                grad[p, 0] += from_left[p]
            ups[p, j] = copies.start(grad.at[p, j, below], from_up.at[p, j], down)
            downs[p, j] = copies.start(grad.at[p, j, top], from_down.at[p, j], up)
        if j == 1:
            reduce.scatter_tiles()
    middles = [copies.start(grad.at[p, 0, middle], from_right.at[p], left) for p in every]
    reduce.sum_column()
    reduce.gather_tiles()
    corners = {}
    for j in [0] + list(range(1, last)):
        for p in every:
            ups[p, j].wait_recv()
            downs[p, j].wait_recv()
            ups[p, j].wait_send()
            downs[p, j].wait_send()
            if j == 0:
                grad[p, j, top] += from_up[p, j]
                grad[p, j, below] += from_down[p, j]
                for k, rows in enumerate((top, below)):
                    corners[p, k] = copies.start(grad.at[p, j, rows], from_corner.at[p, k], left)
                new_extended[p, j] = extended[p, j] - STEP_OBJECT * grad[p, j]
            else:
                new = extended[p, j] - STEP_OBJECT * grad[p, j]
                new_extended[p, j] = new
                new_extended[p, j, top] -= STEP_OBJECT * from_up[p, j]
                new_extended[p, j, below] -= STEP_OBJECT * from_down[p, j]
    reduce.gather_pair()
    for p in every:
        middles[p].wait_recv()
        new_extended[p, last, middle] = extended[p, last, middle] - STEP_OBJECT * from_right[p]
        for k, rows in enumerate((top, below)):
            corners[p, k].wait_recv()
            new_extended[p, last, rows] = extended[p, last, rows] - STEP_OBJECT * from_corner[p, k]
    positions = 8 * tiles * cols
    new_probe[...] = probe[...] - (1.0 / positions) * reduce.result()
    waited = {id(copy) for copy in list(ups.values()) + list(downs.values())}
    for copy in copies.started:
        if id(copy) not in waited:
            copy.wait_send()


def exchange(grad, extended, grad_probe, probe, tiles, cols):
    planes, count, tall, size = grad.shape
    last = count - 1
    height = tall - size
    rows, lanes = probe.shape
    needed = ProbeSum.copies_needed(tiles, cols) + planes * (1 + 2 * last + 1 + 2)
    return pl.pallas_call(
        functools.partial(exchange_kernel, tiles, cols),
        out_shape=[
            jax.ShapeDtypeStruct(extended.shape, f32),
            jax.ShapeDtypeStruct(probe.shape, f32),
        ],
        in_specs=[VMEM_SPEC] * 4,
        out_specs=[VMEM_SPEC] * 2,
        scratch_shapes=[
            pltpu.VMEM((planes, tall, size), f32),
            pltpu.VMEM((planes, height - size, size), f32),
            pltpu.VMEM((planes, last, size, size), f32),
            pltpu.VMEM((planes, last, size, size), f32),
            pltpu.VMEM((planes, 2, size, size), f32),
            *ProbeSum.scratch(rows, lanes, tiles, cols),
            pltpu.SemaphoreType.DMA((needed,)),
            pltpu.SemaphoreType.DMA((needed,)),
        ],
        compiler_params=pltpu.CompilerParams(
            collective_id=1, has_side_effects=True, vmem_limit_bytes=VMEM_LIMIT
        ),
        name="exchange",
    )(grad, extended, grad_probe, probe)


def narrow_kernel(
    tiles,
    cols,
    grad,
    extended,
    grad_probe,
    probe,
    new_field,
    new_probe,
    from_left,
    from_up,
    pair,
    pieces,
    column,
    halves,
    send,
    recv,
):
    planes, count, tall, size = grad.shape
    last = count - 1
    height = tall - size
    top, own, below = pl.ds(0, size), pl.ds(0, height), pl.ds(height, size)
    place = Place(tiles, cols)
    greet(met(place))
    copies = Copies(send, recv)
    down, right = place.at(1, 0), place.at(0, 1)
    reduce = ProbeSum(place, copies, grad_probe, pair, pieces, column, halves)
    every = range(planes)
    reduce.scatter_pair()
    sides = [copies.start(grad.at[p, last], from_left.at[p], right) for p in every]
    ups = {}
    for j in list(range(1, last)) + [0]:
        for p in every:
            if j == 0:
                sides[p].wait_recv()
                grad[p, 0] += from_left[p]
            ups[p, j] = copies.start(grad.at[p, j, below], from_up.at[p, j], down)
        if j == 1:
            reduce.scatter_tiles()
    for j in range(last):
        for p in every:
            new_field[p, :, pl.ds(j * size, size)] = extended[p, j, own] - STEP_OBJECT * grad[p, j, own]
    reduce.sum_column()
    reduce.gather_tiles()
    reduce.gather_pair()
    for j in list(range(1, last)) + [0]:
        for p in every:
            ups[p, j].wait_recv()
            new_field[p, top, pl.ds(j * size, size)] -= STEP_OBJECT * from_up[p, j]
    positions = 8 * tiles * cols
    new_probe[...] = probe[...] - (1.0 / positions) * reduce.result()
    copies.finish()


def narrow(grad, extended, grad_probe, probe, tiles, cols):
    planes, count, tall, size = grad.shape
    last = count - 1
    height = tall - size
    rows, lanes = probe.shape
    needed = ProbeSum.copies_needed(tiles, cols) + planes * (1 + last)
    return pl.pallas_call(
        functools.partial(narrow_kernel, tiles, cols),
        out_shape=[
            jax.ShapeDtypeStruct((planes, height, last * size), f32),
            jax.ShapeDtypeStruct(probe.shape, f32),
        ],
        in_specs=[VMEM_SPEC] * 4,
        out_specs=[VMEM_SPEC] * 2,
        scratch_shapes=[
            pltpu.VMEM((planes, tall, size), f32),
            pltpu.VMEM((planes, last, size, size), f32),
            *ProbeSum.scratch(rows, lanes, tiles, cols),
            pltpu.SemaphoreType.DMA((needed,)),
            pltpu.SemaphoreType.DMA((needed,)),
        ],
        compiler_params=pltpu.CompilerParams(
            collective_id=2, has_side_effects=True, vmem_limit_bytes=VMEM_LIMIT
        ),
        name="narrow",
    )(grad, extended, grad_probe, probe)


def local(table, tiles, cols, object_field, probe, row_offsets, col_offsets, counts, measured):
    size = probe.shape[-1]
    height, width = object_field.shape[2:]
    slots = row_offsets.shape[-1]
    rows = row_offsets.reshape(slots)
    columns = col_offsets.reshape(slots)
    count = counts.reshape(1)
    data = measured.reshape(slots, size, size)
    field = object_field.reshape(4, height, width)
    beam = probe
    flat = (probe.shape[0] * probe.shape[1] * size, size)
    extended = widen(field, size, tiles, cols)
    for sweep in range(ITERS):
        grad, grad_beam = gradients(rows, columns, count, extended, beam, data, table)
        combine = narrow if sweep == ITERS - 1 else exchange
        extended, beam = combine(
            grad, extended, grad_beam.reshape(flat), beam.reshape(flat), tiles, cols
        )
        beam = beam.reshape(probe.shape)
    return extended.reshape(object_field.shape), beam


def solution(mesh):
    table = jnp.asarray(transform_tables(128))
    tiles, cols = mesh.shape["tiles"], mesh.shape["cols"]
    in_specs = (
        P(None, None, "tiles", "cols"),
        P(),
        P("tiles", "cols", None),
        P("tiles", "cols", None),
        P("tiles", "cols"),
        P("tiles", "cols", None, None, None),
    )
    out_specs = (P(None, None, "tiles", "cols"), P())
    body = functools.partial(local, table, tiles, cols)
    return jax.shard_map(body, mesh=mesh, in_specs=in_specs, out_specs=out_specs, check_vma=False)
```

time: 1070 us -> 135 us (0.13)
  starting transfers between devices: 547 us -> 0 us
  waiting for transfers between devices: 383 us -> 0 us
  Pallas kernels: 0 us -> 130 us
  matrix products: 52 us -> 0 us
  local copies, waits for them, and re-layouts: 35 us -> 3.14 us
  other arithmetic: 19.7 us -> 0 us
  between operations: 14.8 us -> 1.31 us
  loops' own time: 11.8 us -> 0 us
    ppermute x16 -> x0, starting transfers between devices: 547 us -> none  [from_behind(): return lax.ppermute(block, axis, route)]
    psum x2 -> x0, waiting for transfers between devices: 358 us -> none  [local(): grad_beam = lax.psum(grad_beam, ('tiles', 'cols'))]
    pallas_call x0 -> x5, Pallas kernels: none -> 130 us  [the longest x1 44.1 us: exchange(): pl.pallas_call(functools.partial(exchange_kernel, tiles, cols), out_shape...]
    dot_general x48 -> x0, matrix products: 52 us -> none  [the longest x12 13.1 us: transform(): jnp.einsum('zmab,bc->zmac', middle, real_table, precision=exact)]
    ppermute x16 -> x0, waiting for transfers between devices: 24.3 us -> none  [from_behind(): return lax.ppermute(block, axis, route)]
    another operation x2 -> x0, loops' own time: 11.8 us -> none  [gradients(): grad_ext, grad_beam = lax.fori_loop(0, count, visit, start)]
    slice x15 -> x0, local copies, waits for them, and re-layouts: 11.6 us -> none  [the longest x2 3.12 us: narrow(): below = from_behind(grad_ext[:, :, tile_rows:, :tile_cols], 'tiles', 1)]
  transfers between devices with their start and end apart: 18 -> 0, of which waited for: 8 -> 0; matrix products, arithmetic and copies ran while one was open for 1% -> 0% of each run, Pallas kernels for 0% -> 0%
where the time goes in v1:
time: 135 us
  Pallas kernels  130 us (96%)
  local copies, waits for them, and re-layouts  3.14 us (2%)
    pallas_call x1, Pallas kernels, exchange(): pl.pallas_call(functools.partial(exchange_kernel, tiles, cols), out_shape...  44.1 us
    pallas_call x1, Pallas kernels, narrow(): pl.pallas_call(functools.partial(narrow_kernel, tiles, cols), out_shape=[...  38.2 us
    pallas_call x1, Pallas kernels, widen(): pl.pallas_call(functools.partial(widen_kernel, tiles, cols, size), out_sh...  24.1 us
    pallas_call x2, Pallas kernels, gradients(): pl.pallas_call(gradient_kernel, out_shape=[jax.ShapeDtypeStruct(extended....  23.8 us
    unnamed x4, local copies, waits for them, and re-layouts  3.14 us

profile of v1, /device:TPU:1, one launch (start us, length us, event | category | flops | bytes accessed | tf_op | source)
XLA Modules:
  0.0 134.6 jit_solution(12706338165867805060)
XLA Ops:
  1.3 24.1 %widen.1.extended = f32[4,3,384,128]{3,2,1,0:T(8,128)} custom-call(f32[4,256,256]{2,1,0:T(8,128)} %bitcast.13), custom_call_target="tpu_custom_call" | custom-call | tf_op jit(solution)/shard_map/widen/pallas_call | solution.py:246
  25.4 11.8 %gradients.2 = (f32[4,3,384,128]{3,2,1,0:T(8,128)}, f32[2,4,128,128]{3,2,1,0:T(8,128)}) custom-call(s32[8]{0:T(128)} %bitcast.22, s32[8]{0:T(128)} %bitcast.24, s32[1]{0:T(128)} %bitcast.11.counts, f32[4,3,384,128]{3,2,1,0:T(8,128)} %widen.1.extended, f32[2,4,128,128]{3,2,1,0:T(8,128)} %probe.1, f32[8,128,128]{2,1,0:T(8,128)} %bitcast.20, ...), custom_call_target="tpu_custom_call" | custom-call | flops 12884901888 | bytes 8388608 | tf_op jit(solution)/shard_map/gradients/pallas_call | solution.py:155
  37.2 44.1 %exchange.1 = (f32[4,3,384,128]{3,2,1,0:T(8,128)}, f32[1024,128]{1,0:T(8,128)}) custom-call(f32[4,3,384,128]{3,2,1,0:T(8,128)} %get-tuple-element.10.grad, f32[4,3,384,128]{3,2,1,0:T(8,128)} %widen.1.extended, f32[1024,128]{1,0:T(8,128)} %bitcast.19, f32[1024,128]{1,0:T(8,128)} %bitcast.16), custom_call_target="tpu_custom_call" | custom-call | tf_op jit(solution)/shard_map/exchange/pallas_call | solution.py:440
  81.2 12.0 %gradients.3 = (f32[4,3,384,128]{3,2,1,0:T(8,128)}, f32[2,4,128,128]{3,2,1,0:T(8,128)}) custom-call(s32[8]{0:T(128)} %bitcast.23, s32[8]{0:T(128)} %bitcast.25, s32[1]{0:T(128)} %bitcast.12.counts, f32[4,3,384,128]{3,2,1,0:T(8,128)} %get-tuple-element.12.extended, f32[2,4,128,128]{3,2,1,0:T(8,128)} %bitcast.17, f32[8,128,128]{2,1,0:T(8,128)} %bitcast.21, ...), custom_call_target="tpu_custom_call" | custom-call | flops 12884901888 | bytes 8388608 | tf_op jit(solution)/shard_map/gradients/pallas_call | solution.py:155
  93.2 38.2 %narrow.1 = (f32[4,256,256]{2,1,0:T(8,128)}, f32[1024,128]{1,0:T(8,128)}) custom-call(f32[4,3,384,128]{3,2,1,0:T(8,128)} %get-tuple-element.14.grad, f32[4,3,384,128]{3,2,1,0:T(8,128)} %get-tuple-element.12.extended, f32[1024,128]{1,0:T(8,128)} %bitcast.18, f32[1024,128]{1,0:T(8,128)} %get-tuple-element.13.probe), custom_call_target="tpu_custom_call" | custom-call | tf_op jit(solution)/shard_map/narrow/pallas_call | solution.py:525
  131.5 0.0 copy-start
  131.5 2.3 %copy.12 = f32[2,2,256,256]{3,2,1,0:T(8,128)} copy(f32[2,2,256,256]{3,2,1,0:T(8,128)} %bitcast.14) | data formatting | bytes 2097152
  133.8 0.0 copy-done
  133.8 0.8 copy.13
Async XLA Ops:
  131.5 2.4 %copy-start = (f32[1024,128]{1,0:T(8,128)S(1)}, f32[1024,128]{1,0:T(8,128)}, u32[]{:S(2)}) copy-start(f32[1024,128]{1,0:T(8,128)} %get-tuple-element.17) | copy-start | bytes 1572868

commit v2 on v1

v2 whole, which is shorter than its diff:
```python
import functools
import math

import jax
import jax.numpy as jnp
import ml_dtypes
import numpy as np
from jax import lax
from jax.experimental import pallas as pl
from jax.experimental.pallas import tpu as pltpu
from jax.sharding import PartitionSpec as P

ITERS = 2
STEP_OBJECT = 0.25
f32, bf16 = jnp.float32, jnp.bfloat16
MESH = pl.DeviceIdType.MESH
VMEM_LIMIT = 56 * 2**20

A_PLUS, A_MINUS, F_PLUS, F_MINUS = 0, 2, 4, 6


def split_table(table):
    high = table.astype(np.float32).astype(ml_dtypes.bfloat16)
    low = (table - high.astype(np.float64)).astype(np.float32).astype(ml_dtypes.bfloat16)
    return [high, low]


def transform_tables(size):
    line = np.arange(size)
    dft = np.exp(-2j * np.pi * (np.outer(line, line) % size) / size) / math.sqrt(size)
    freq = np.where(line < size // 2, line, line - size)
    chirp = np.exp(-2j * np.pi * ((freq * freq) % (4 * size)) / (4 * size))
    propagator = np.conj(dft) @ (chirp[:, None] * dft)
    parts = []
    for matrix in (propagator, dft):
        real, imag = matrix.real, matrix.imag
        plus = np.block([[real, imag], [-imag, real]])
        parts += split_table(plus) + split_table(plus.T)
    return np.stack(parts)


def split(value):
    high = value.astype(bf16)
    return high, (value - high.astype(f32)).astype(bf16)


def product(first, second):
    dot = functools.partial(jnp.dot, preferred_element_type=f32)
    return dot(first[0], second[0]) + (dot(first[1], second[0]) + dot(first[0], second[1]))


def two_sided(fields, table, left, right):
    n = fields[0][0].shape[0]
    modes = range(len(fields))
    stacked = [jnp.concatenate(field, axis=0) for field in fields]
    middle = product((table[left], table[left + 1]), split(jnp.concatenate(stacked, axis=1)))
    columns = [middle[:, n * m : n * m + n] for m in modes]
    beside = [jnp.concatenate([c[:n], c[n:]], axis=1) for c in columns]
    result = product(split(jnp.concatenate(beside, axis=0)), (table[right], table[right + 1]))
    rows = [result[n * m : n * m + n] for m in modes]
    return [(row[:, :n], row[:, n:]) for row in rows]


def times(a, b):
    return (a[0] * b[0] - a[1] * b[1], a[0] * b[1] + a[1] * b[0])


def conj_times(a, b):
    return (a[0] * b[0] + a[1] * b[1], a[0] * b[1] - a[1] * b[0])


def total(terms):
    real, imag = terms[0]
    for term in terms[1:]:
        real, imag = real + term[0], imag + term[1]
    return real, imag


GROUP = 4


def add_gradients(rows, cols, counts, measured, extended, beam, table, grad, grad_beam, slots):
    planes, count_blocks, tall, n = grad.shape
    modes = range(beam.shape[0] // (2 * n))
    part = len(modes) * n
    grad[...] = jnp.zeros_like(grad)
    grad_beam[...] = jnp.zeros_like(grad_beam)
    lane = lax.broadcasted_iota(jnp.int32, (n, n), 1)
    offset = lax.broadcasted_iota(jnp.int32, (tall, n), 0) - lax.broadcasted_iota(
        jnp.int32, (tall, n), 1
    )
    count = counts[0]
    real_rows = [pl.ds(m * n, n) for m in modes]
    imag_rows = [pl.ds(part + m * n, n) for m in modes]

    def visit(step, carry):
        beams = [(beam[a], beam[b]) for a, b in zip(real_rows, imag_rows)]
        spots = []
        for k in range(GROUP):
            slot = step * GROUP + k
            live = slot < count
            row = jnp.where(live, rows[slot], 0)
            col = jnp.where(live, cols[slot], 0)
            block = lax.shift_right_logical(col, 7)
            weight = jnp.where(live, 1.0, 0.0).astype(f32)
            spots.append((slot, weight, row, block, col - block * n))

        def window(plane, spot):
            _, _, row, block, shift = spot
            back = jnp.bitwise_and(n - shift, n - 1)
            near = pltpu.roll(extended[plane, block, pl.ds(row, n), :], back, 1)
            far = pltpu.roll(extended[plane, block + 1, pl.ds(row, n), :], back, 1)
            return jnp.where(lane < n - shift, near, far)

        first = [(window(0, s), window(2, s)) for s in spots]
        spread = [two_sided([times(b, o) for b in beams], table, A_MINUS, A_PLUS) for o in first]
        second = [(window(1, s), window(3, s)) for s in spots]
        far = [
            two_sided([times(o, x) for x in fields], table, F_MINUS, F_PLUS)
            for o, fields in zip(second, spread)
        ]
        residual = []
        for spot, fields in zip(spots, far):
            intensity = sum(y[0] * y[0] + y[1] * y[1] for y in fields)
            residual.append((intensity - measured[spot[0]]) * spot[1])
        back = [
            two_sided([(r * y[0], r * y[1]) for y in fields], table, F_PLUS, F_MINUS)
            for r, fields in zip(residual, far)
        ]
        grad_second = [
            total([conj_times(x, g) for x, g in zip(fields, backs)])
            for fields, backs in zip(spread, back)
        ]
        back = [
            two_sided([conj_times(o, g) for g in backs], table, A_PLUS, A_MINUS)
            for o, backs in zip(second, back)
        ]
        grad_first = [total([conj_times(b, g) for b, g in zip(beams, backs)]) for backs in back]
        for m in modes:
            real, imag = total([conj_times(o, backs[m]) for o, backs in zip(first, back)])
            grad_beam[real_rows[m]] += real
            grad_beam[imag_rows[m]] += imag
        put, pieces = [], [[] for _ in range(count_blocks)]
        for (_, _, row, block, shift), g0, g1 in zip(spots, grad_first, grad_second):
            put += [jnp.where(offset == row, 1.0, 0.0).astype(bf16)] * 2
            kept = lane >= shift
            beside = [[] for _ in range(count_blocks)]
            for value in (g0[0], g1[0], g0[1], g1[1]):
                moved = pltpu.roll(value, shift, 1)
                near, over = jnp.where(kept, moved, 0.0), jnp.where(kept, 0.0, moved)
                for b in range(count_blocks):
                    if b == 0:
                        placed = jnp.where(block == 0, near, 0.0)
                    elif b == count_blocks - 1:
                        placed = jnp.where(block == b - 1, over, 0.0)
                    else:
                        placed = jnp.where(block == b, near, jnp.where(block == b - 1, over, 0.0))
                    beside[b].append(placed)
            for b in range(count_blocks):
                pieces[b] += split(jnp.concatenate(beside[b], axis=1))
        put = jnp.concatenate(put, axis=1)
        for b in range(count_blocks):
            sums = jnp.dot(put, jnp.concatenate(pieces[b], axis=0), preferred_element_type=f32)
            for p in range(planes):
                grad[p, b] += sums[:, p * n : p * n + n]
        return carry

    lax.fori_loop(0, slots // GROUP, visit, 0)


class Place:
    def __init__(self, tiles, cols):
        self.tiles, self.cols = tiles, cols
        self.t, self.c = lax.axis_index("tiles"), lax.axis_index("cols")

    def at(self, down, right):
        return (
            lax.rem(self.t + (down + self.tiles), self.tiles),
            lax.rem(self.c + (right + self.cols), self.cols),
        )


def greet(devices):
    barrier = pltpu.get_barrier_semaphore()
    for device in devices:
        pl.semaphore_signal(barrier, inc=1, device_id=device, device_id_type=MESH)
    pl.semaphore_wait(barrier, len(devices))


class Copies:
    def __init__(self, send, recv):
        self.send, self.recv, self.used, self.started = send, recv, 0, []

    def start(self, source, target, device):
        k = self.used
        self.used += 1
        copy = pltpu.make_async_remote_copy(
            src_ref=source,
            dst_ref=target,
            send_sem=self.send.at[k],
            recv_sem=self.recv.at[k],
            device_id=device,
            device_id_type=MESH,
        )
        copy.start()
        self.started.append(copy)
        return copy

    def sent(self, copy):
        copy.wait_send()
        self.started = [other for other in self.started if other is not copy]

    def finish(self):
        for copy in self.started:
            copy.wait_send()
        self.started = []


class ProbeSum:
    def __init__(self, place, copies, grad, pair, pieces, column, halves):
        self.place, self.copies = place, copies
        self.grad, self.pair, self.pieces, self.column, self.halves = grad, pair, pieces, column, halves
        self.half = grad.shape[0] // 2
        self.piece = self.half // place.tiles
        self.core = lax.rem(place.c, 2)
        self.partner = (place.t, place.c + 1 - 2 * self.core)
        self.mine = pl.ds(self.core * self.half, self.half)
        self.others = pl.ds((1 - self.core) * self.half, self.half)

    def scatter_pair(self):
        self.step = self.copies.start(self.grad.at[self.others], self.pair, self.partner)

    def scatter_tiles(self):
        self.step.wait_recv()
        self.grad[self.mine] += self.pair[...]
        place, piece = self.place, self.piece
        self.steps = []
        for k in range(1, place.tiles):
            peer = lax.rem(place.t + k, place.tiles)
            source = self.grad.at[pl.ds(self.core * self.half + peer * piece, piece)]
            self.steps.append(
                self.copies.start(source, self.pieces.at[k - 1], (peer, place.c))
            )

    def sum_column(self):
        place, piece = self.place, self.piece
        value = self.grad[pl.ds(self.core * self.half + place.t * piece, piece)]
        for k, step in enumerate(self.steps):
            step.wait_recv()
            value += self.pieces[k]
        chips = place.cols // 2
        chip = place.c // 2
        self.column[chip] = value
        self.steps = []
        for k in range(1, chips):
            peer = (place.t, lax.rem(place.c + 2 * k, place.cols))
            self.steps.append(
                self.copies.start(self.column.at[chip], self.column.at[chip], peer)
            )

    def gather_tiles(self):
        for step in self.steps:
            step.wait_recv()
        place, piece = self.place, self.piece
        value = self.column[0]
        for k in range(1, place.cols // 2):
            value += self.column[k]
        own = pl.ds(self.core * self.half + place.t * piece, piece)
        self.halves[own] = value
        self.steps = []
        for k in range(1, place.tiles):
            peer = lax.rem(place.t + k, place.tiles)
            self.steps.append(
                self.copies.start(self.halves.at[own], self.halves.at[own], (peer, place.c))
            )

    def gather_pair(self):
        for step in self.steps:
            step.wait_recv()
        self.step = self.copies.start(
            self.halves.at[self.mine], self.halves.at[self.mine], self.partner
        )

    def result(self):
        self.step.wait_recv()
        return self.halves[...]

    @staticmethod
    def copies_needed(tiles, cols):
        return 2 * tiles + cols // 2 - 1

    @staticmethod
    def scratch(rows, lanes, tiles, cols):
        half = rows // 2
        piece = half // tiles
        return [
            pltpu.VMEM((half, lanes), f32),
            pltpu.VMEM((tiles - 1, piece, lanes), f32),
            pltpu.VMEM((cols // 2, piece, lanes), f32),
            pltpu.VMEM((rows, lanes), f32),
        ]


def met(place):
    devices = [place.at(k, 0) for k in range(1, place.tiles)]
    return devices + [
        place.at(0, k) for k in range(1, place.cols) if k % 2 == 0 or k in (1, place.cols - 1)
    ]


def met(place):
    devices = [place.at(k, 0) for k in range(1, place.tiles)]
    return devices + [
        place.at(0, k) for k in range(1, place.cols) if k % 2 == 0 or k in (1, place.cols - 1)
    ]


def program_kernel(
    tiles,
    cols,
    rows,
    columns,
    counts,
    field,
    probe_hbm,
    measured_hbm,
    table_hbm,
    new_field,
    new_probe,
    extended,
    grad,
    beam,
    grad_beam,
    measured,
    table,
    from_left,
    from_up,
    from_right,
    from_down,
    from_corner,
    *rest,
):
    sums, (local_sem, send, recv) = rest[:-3], rest[-3:]
    sums = [sums[: len(sums) // 2], sums[len(sums) // 2 :]]
    planes, count, tall, size = grad.shape
    last = count - 1
    height = tall - size
    slots = measured.shape[0]
    step_probe = 1.0 / (slots * tiles * cols)
    top, middle, below = pl.ds(0, size), pl.ds(size, height - size), pl.ds(height, size)
    own = pl.ds(0, height)
    block = [pl.ds(j * size, size) for j in range(last)]
    every = range(planes)
    place = Place(tiles, cols)
    copies = Copies(send, recv)
    up, down, left, right = place.at(-1, 0), place.at(1, 0), place.at(0, -1), place.at(0, 1)

    loads = [(field.at[:, :, block[j]], extended.at[:, j, own, :]) for j in range(last)]
    loads += [(probe_hbm, beam), (table_hbm, table), (measured_hbm, measured)]
    loads = [
        pltpu.make_async_copy(source, target, local_sem.at[k])
        for k, (source, target) in enumerate(loads)
    ]
    for load in loads:
        load.start()
    greet(met(place))

    halos = {
        (p, j): copies.start(field.at[p, top, block[j]], extended.at[p, j, below], up)
        for j in range(last)
        for p in every
    }
    sides = [
        copies.start(field.at[p, :, block[0]], extended.at[p, last, own], left) for p in every
    ]
    corners = []
    for p in every:
        halos[p, 0].wait_recv()
        corners.append(
            copies.start(extended.at[p, 0, below], extended.at[p, last, below], left)
        )
    for load in loads:
        load.wait()
    for copy in list(halos.values())[planes:] + sides + corners:
        copy.wait_recv()
    copies.finish()

    for sweep in range(ITERS):
        add_gradients(
            rows, columns, counts, measured, extended, beam, table, grad, grad_beam, slots
        )
        final = sweep == ITERS - 1
        reduce = ProbeSum(place, copies, grad_beam, *sums[sweep])
        reduce.scatter_pair()
        sides = [
            copies.start(grad.at[p, last], from_left.at[sweep, p], right) for p in every
        ]
        ups, downs = {}, {}

        def send_rows(p, j):
            ups[p, j] = copies.start(grad.at[p, j, below], from_up.at[sweep, p, j], down)
            if not final:
                downs[p, j] = copies.start(grad.at[p, j, top], from_down.at[p, j], up)

        for j in range(1, last):
            for p in every:
                send_rows(p, j)
        reduce.scatter_tiles()
        for p in every:
            sides[p].wait_recv()
            grad[p, 0] += from_left[sweep, p]
            send_rows(p, 0)
        if final:
            reduce.sum_column()
            for j in range(last):
                for p in every:
                    new_field[p, :, block[j]] = extended[p, j, own] - STEP_OBJECT * grad[p, j, own]
            reduce.gather_tiles()
            for j in list(range(1, last)) + [0]:
                for p in every:
                    ups[p, j].wait_recv()
                    new_field[p, top, block[j]] -= STEP_OBJECT * from_up[sweep, p, j]
            reduce.gather_pair()
            new_probe[...] = beam[...] - step_probe * reduce.result()
        else:
            middles = [
                copies.start(grad.at[p, 0, middle], from_right.at[p], left) for p in every
            ]
            reduce.sum_column()
            reduce.gather_tiles()
            corners = {}
            for p in every:
                copies.sent(ups[p, 0])
                copies.sent(downs[p, 0])
                for way, landed, lines in ((ups, from_up.at[sweep], top), (downs, from_down, below)):
                    way[p, 0].wait_recv()
                    grad[p, 0, lines] += landed[p, 0]
                for k, lines in enumerate((top, below)):
                    corners[p, k] = copies.start(
                        grad.at[p, 0, lines], from_corner.at[p, k], left
                    )
                extended[p, 0] -= STEP_OBJECT * grad[p, 0]
            reduce.gather_pair()
            for j in range(1, last):
                for p in every:
                    ups[p, j].wait_recv()
                    downs[p, j].wait_recv()
                    extended[p, j, middle] -= STEP_OBJECT * grad[p, j, middle]
                    extended[p, j, top] -= STEP_OBJECT * (grad[p, j, top] + from_up[sweep, p, j])
                    extended[p, j, below] -= STEP_OBJECT * (grad[p, j, below] + from_down[p, j])
            for p in every:
                middles[p].wait_recv()
                extended[p, last, middle] -= STEP_OBJECT * from_right[p]
                for k, lines in enumerate((top, below)):
                    corners[p, k].wait_recv()
                    extended[p, last, lines] -= STEP_OBJECT * from_corner[p, k]
            beam[...] -= step_probe * reduce.result()
        copies.finish()


def local(table, tiles, cols, object_field, probe, row_offsets, col_offsets, counts, measured):
    size = probe.shape[-1]
    height, width = object_field.shape[2:]
    slots = row_offsets.shape[-1]
    field = object_field.reshape(4, height, width)
    flat = (probe.shape[0] * probe.shape[1] * size, size)
    planes, last, tall = 4, width // size, height + size
    needed = planes * (2 * last + 2) + ITERS * ProbeSum.copies_needed(tiles, cols)
    needed += planes * (1 + 2 * last + 1 + 2) + planes * (1 + last)
    work = ITERS * slots * probe.shape[1] * 8 * 3 * 2 * 256 * 256 * 128
    smem = pl.BlockSpec(memory_space=pltpu.SMEM)
    hbm = pl.BlockSpec(memory_space=pl.ANY)
    vmem = pl.BlockSpec(memory_space=pltpu.VMEM)
    new_field, new_probe = pl.pallas_call(
        functools.partial(program_kernel, tiles, cols),
        out_shape=[jax.ShapeDtypeStruct(field.shape, f32), jax.ShapeDtypeStruct(flat, f32)],
        in_specs=[smem] * 3 + [hbm] * 4,
        out_specs=[vmem] * 2,
        scratch_shapes=[
            pltpu.VMEM((planes, last + 1, tall, size), f32),
            pltpu.VMEM((planes, last + 1, tall, size), f32),
            pltpu.VMEM(flat, f32),
            pltpu.VMEM(flat, f32),
            pltpu.VMEM((slots, size, size), f32),
            pltpu.VMEM(table.shape, bf16),
            pltpu.VMEM((ITERS, planes, tall, size), f32),
            pltpu.VMEM((ITERS, planes, last, size, size), f32),
            pltpu.VMEM((planes, height - size, size), f32),
            pltpu.VMEM((planes, last, size, size), f32),
            pltpu.VMEM((planes, 2, size, size), f32),
            *ProbeSum.scratch(*flat, tiles, cols),
            *ProbeSum.scratch(*flat, tiles, cols),
            pltpu.SemaphoreType.DMA((last + 3,)),
            pltpu.SemaphoreType.DMA((needed,)),
            pltpu.SemaphoreType.DMA((needed,)),
        ],
        compiler_params=pltpu.CompilerParams(
            collective_id=0, has_side_effects=True, vmem_limit_bytes=VMEM_LIMIT
        ),
        cost_estimate=pl.CostEstimate(flops=work, bytes_accessed=5 * 2**20, transcendentals=0),
        name="ptychography",
    )(
        row_offsets.reshape(slots),
        col_offsets.reshape(slots),
        counts.reshape(1),
        field,
        probe.reshape(flat),
        measured.reshape(slots, size, size),
        table,
    )
    return new_field.reshape(object_field.shape), new_probe.reshape(probe.shape)


def solution(mesh):
    table = jnp.asarray(transform_tables(128))
    tiles, cols = mesh.shape["tiles"], mesh.shape["cols"]
    in_specs = (
        P(None, None, "tiles", "cols"),
        P(),
        P("tiles", "cols", None),
        P("tiles", "cols", None),
        P("tiles", "cols"),
        P("tiles", "cols", None, None, None),
    )
    out_specs = (P(None, None, "tiles", "cols"), P())
    body = functools.partial(local, table, tiles, cols)
    return jax.shard_map(body, mesh=mesh, in_specs=in_specs, out_specs=out_specs, check_vma=False)
```

time: 135 us -> 118 us (0.87)
  Pallas kernels: 130 us -> 113 us
    pallas_call x5 -> x1, Pallas kernels: 130 us -> 113 us  [local(): pl.pallas_call(functools.partial(program_kernel, tiles, cols), out_shape=...]
where the time goes in v2:
time: 118 us
  Pallas kernels  113 us (96%)
  local copies, waits for them, and re-layouts  3.14 us (3%)
  between operations  1.29 us (1%)
    pallas_call x1, Pallas kernels, local(): pl.pallas_call(functools.partial(program_kernel, tiles, cols), out_shape=...  113 us
    unnamed x4, local copies, waits for them, and re-layouts  3.14 us

profile of v2, /device:TPU:1, one launch (start us, length us, event | category | flops | bytes accessed | tf_op | source)
XLA Modules:
  0.0 117.8 jit_solution(16111451238171736301)
XLA Ops:
  1.3 113.4 %ptychography.1 = (f32[4,256,256]{2,1,0:T(8,128)}, f32[1024,128]{1,0:T(8,128)}) custom-call(s32[8]{0:T(128)} %bitcast.14, s32[8]{0:T(128)} %bitcast.15, s32[1]{0:T(128)} %bitcast.8.counts, f32[4,256,256]{2,1,0:T(8,128)} %bitcast.11, f32[1024,128]{1,0:T(8,128)} %bitcast.12, f32[8,128,128]{2,1,0:T(8,128)} %bitcast.13, bf16[8,256,256]{2,1,0:T(8,128)(2,1)} %constant.2.clone.table_hbm), custom_call_target="tpu_custom_call" | custom-call | flops 25769803776 | bytes 5242880 | tf_op jit(solution)/shard_map/ptychography/pallas_call | solution.py:474
  114.7 0.0 copy-start
  114.7 2.3 %copy.12 = f32[2,2,256,256]{3,2,1,0:T(8,128)} copy(f32[2,2,256,256]{3,2,1,0:T(8,128)} %bitcast.9) | data formatting | bytes 2097152
  117.0 0.0 copy-done
  117.0 0.8 copy.13
Async XLA Ops:
  114.7 2.4 %copy-start = (f32[1024,128]{1,0:T(8,128)S(1)}, f32[1024,128]{1,0:T(8,128)}, u32[]{:S(2)}) copy-start(f32[1024,128]{1,0:T(8,128)} %get-tuple-element.5) | copy-start | bytes 1572868

commit v3 on v2

--- a/solution.py
+++ b/solution.py
@@ -79,93 +79,138 @@
 GROUP = 4
 
 
-def add_gradients(rows, cols, counts, measured, extended, beam, table, grad, grad_beam, slots):
-    planes, count_blocks, tall, n = grad.shape
-    modes = range(beam.shape[0] // (2 * n))
-    part = len(modes) * n
-    grad[...] = jnp.zeros_like(grad)
-    grad_beam[...] = jnp.zeros_like(grad_beam)
-    lane = lax.broadcasted_iota(jnp.int32, (n, n), 1)
-    offset = lax.broadcasted_iota(jnp.int32, (tall, n), 0) - lax.broadcasted_iota(
-        jnp.int32, (tall, n), 1
-    )
-    count = counts[0]
-    real_rows = [pl.ds(m * n, n) for m in modes]
-    imag_rows = [pl.ds(part + m * n, n) for m in modes]
-
-    def visit(step, carry):
-        beams = [(beam[a], beam[b]) for a, b in zip(real_rows, imag_rows)]
-        spots = []
+class Positions:
+    def __init__(self, refs, n, slots):
+        self.rows, self.cols, self.counts, self.measured = refs[:4]
+        self.extended, self.beam, self.table, self.grad, self.grad_beam = refs[4:9]
+        self.windows, self.spread, self.back, self.patches = refs[9:]
+        self.n, self.slots = n, slots
+        self.modes = range(self.spread.shape[1])
+        self.groups = slots // GROUP
+
+    def beams(self):
+        n, part = self.n, len(self.modes) * self.n
+        return [(self.beam[pl.ds(m * n, n)], self.beam[pl.ds(part + m * n, n)]) for m in self.modes]
+
+    def spots(self, step):
+        found = []
         for k in range(GROUP):
             slot = step * GROUP + k
-            live = slot < count
-            row = jnp.where(live, rows[slot], 0)
-            col = jnp.where(live, cols[slot], 0)
+            live = slot < self.counts[0]
+            row = jnp.where(live, self.rows[slot], 0)
+            col = jnp.where(live, self.cols[slot], 0)
             block = lax.shift_right_logical(col, 7)
             weight = jnp.where(live, 1.0, 0.0).astype(f32)
-            spots.append((slot, weight, row, block, col - block * n))
-
-        def window(plane, spot):
-            _, _, row, block, shift = spot
-            back = jnp.bitwise_and(n - shift, n - 1)
-            near = pltpu.roll(extended[plane, block, pl.ds(row, n), :], back, 1)
-            far = pltpu.roll(extended[plane, block + 1, pl.ds(row, n), :], back, 1)
-            return jnp.where(lane < n - shift, near, far)
-
-        first = [(window(0, s), window(2, s)) for s in spots]
-        spread = [two_sided([times(b, o) for b in beams], table, A_MINUS, A_PLUS) for o in first]
-        second = [(window(1, s), window(3, s)) for s in spots]
+            found.append((slot, weight, row, block, col - block * self.n))
+        return found
+
+    def lane(self):
+        return lax.broadcasted_iota(jnp.int32, (self.n, self.n), 1)
+
+    def window(self, plane, spot):
+        n = self.n
+        _, _, row, block, shift = spot
+        back = jnp.bitwise_and(n - shift, n - 1)
+        near = pltpu.roll(self.extended[plane % 2][plane // 2, block, pl.ds(row, n), :], back, 1)
+        far = pltpu.roll(self.extended[plane % 2][plane // 2, block + 1, pl.ds(row, n), :], back, 1)
+        return jnp.where(self.lane() < n - shift, near, far)
+
+    def propagate(self, step):
+        spots, beams = self.spots(step), self.beams()
+        first = [(self.window(0, s), self.window(2, s)) for s in spots]
+        for spot, field in zip(spots, first):
+            self.windows[spot[0], 0], self.windows[spot[0], 1] = field
+            result = two_sided([times(b, field) for b in beams], self.table, A_MINUS, A_PLUS)
+            for m in self.modes:
+                self.spread[spot[0], m, 0], self.spread[spot[0], m, 1] = result[m]
+
+    def diffract(self, step):
+        spots = self.spots(step)
+        spread = [
+            [(self.spread[s[0], m, 0], self.spread[s[0], m, 1]) for m in self.modes] for s in spots
+        ]
+        second = [(self.window(1, s), self.window(3, s)) for s in spots]
         far = [
-            two_sided([times(o, x) for x in fields], table, F_MINUS, F_PLUS)
+            two_sided([times(o, x) for x in fields], self.table, F_MINUS, F_PLUS)
             for o, fields in zip(second, spread)
         ]
         residual = []
         for spot, fields in zip(spots, far):
             intensity = sum(y[0] * y[0] + y[1] * y[1] for y in fields)
-            residual.append((intensity - measured[spot[0]]) * spot[1])
+            residual.append((intensity - self.measured[spot[0]]) * spot[1])
         back = [
-            two_sided([(r * y[0], r * y[1]) for y in fields], table, F_PLUS, F_MINUS)
+            two_sided([(r * y[0], r * y[1]) for y in fields], self.table, F_PLUS, F_MINUS)
             for r, fields in zip(residual, far)
         ]
-        grad_second = [
+        patches = [
             total([conj_times(x, g) for x, g in zip(fields, backs)])
             for fields, backs in zip(spread, back)
         ]
-        back = [
-            two_sided([conj_times(o, g) for g in backs], table, A_PLUS, A_MINUS)
-            for o, backs in zip(second, back)
-        ]
-        grad_first = [total([conj_times(b, g) for b, g in zip(beams, backs)]) for backs in back]
-        for m in modes:
-            real, imag = total([conj_times(o, backs[m]) for o, backs in zip(first, back)])
-            grad_beam[real_rows[m]] += real
-            grad_beam[imag_rows[m]] += imag
-        put, pieces = [], [[] for _ in range(count_blocks)]
-        for (_, _, row, block, shift), g0, g1 in zip(spots, grad_first, grad_second):
-            put += [jnp.where(offset == row, 1.0, 0.0).astype(bf16)] * 2
-            kept = lane >= shift
-            beside = [[] for _ in range(count_blocks)]
-            for value in (g0[0], g1[0], g0[1], g1[1]):
+        for spot, o, backs in zip(spots, second, back):
+            for m in self.modes:
+                self.back[spot[0], m, 0], self.back[spot[0], m, 1] = conj_times(o, backs[m])
+        self.put(spots, patches, (1, 3), False)
+
+    def return_back(self, step):
+        spots, beams = self.spots(step), self.beams()
+        n, part = self.n, len(self.modes) * self.n
+        back = []
+        for spot in spots:
+            fields = [(self.back[spot[0], m, 0], self.back[spot[0], m, 1]) for m in self.modes]
+            back.append(two_sided(fields, self.table, A_PLUS, A_MINUS))
+        first = [(self.windows[s[0], 0], self.windows[s[0], 1]) for s in spots]
+        for m in self.modes:
+            terms = total([conj_times(o, backs[m]) for o, backs in zip(first, back)])
+            for term, start in zip(terms, (m * n, part + m * n)):
+                if step == 0:
+                    self.grad_beam[pl.ds(start, n)] = term
+                else:
+                    self.grad_beam[pl.ds(start, n)] += term
+        for spot, backs in zip(spots, back):
+            patch = total([conj_times(b, g) for b, g in zip(beams, backs)])
+            self.patches[spot[0], 0], self.patches[spot[0], 1] = patch
+
+    def put_first(self, step):
+        spots = self.spots(step)
+        patches = [(self.patches[s[0], 0], self.patches[s[0], 1]) for s in spots]
+        self.put(spots, patches, (0, 2), step == 0)
+
+    def clear(self, planes):
+        for p in planes:
+            self.grad[p] = jnp.zeros(self.grad.shape[1:], f32)
+
+    def put(self, spots, patches, planes, fresh):
+        n = self.n
+        count, tall = self.grad.shape[1:3]
+        offset = lax.broadcasted_iota(jnp.int32, (tall, n), 0) - lax.broadcasted_iota(
+            jnp.int32, (tall, n), 1
+        )
+        ones, pieces = [], [[] for _ in range(count)]
+        for (_, _, row, block, shift), patch in zip(spots, patches):
+            ones += [jnp.where(offset == row, 1.0, 0.0).astype(bf16)] * 2
+            kept = self.lane() >= shift
+            beside = [[] for _ in range(count)]
+            for value in patch:
                 moved = pltpu.roll(value, shift, 1)
                 near, over = jnp.where(kept, moved, 0.0), jnp.where(kept, 0.0, moved)
-                for b in range(count_blocks):
+                for b in range(count):
                     if b == 0:
                         placed = jnp.where(block == 0, near, 0.0)
-                    elif b == count_blocks - 1:
+                    elif b == count - 1:
                         placed = jnp.where(block == b - 1, over, 0.0)
                     else:
                         placed = jnp.where(block == b, near, jnp.where(block == b - 1, over, 0.0))
                     beside[b].append(placed)
-            for b in range(count_blocks):
+            for b in range(count):
                 pieces[b] += split(jnp.concatenate(beside[b], axis=1))
-        put = jnp.concatenate(put, axis=1)
-        for b in range(count_blocks):
-            sums = jnp.dot(put, jnp.concatenate(pieces[b], axis=0), preferred_element_type=f32)
-            for p in range(planes):
-                grad[p, b] += sums[:, p * n : p * n + n]
-        return carry
-
-    lax.fori_loop(0, slots // GROUP, visit, 0)
+        ones = jnp.concatenate(ones, axis=1)
+        for b in range(count):
+            sums = jnp.dot(ones, jnp.concatenate(pieces[b], axis=0), preferred_element_type=f32)
+            for k, p in enumerate(planes):
+                if fresh:
+                    self.grad[p, b] = sums[:, k * n : k * n + n]
+                else:
+                    self.grad[p, b] += sums[:, k * n : k * n + n]
 
 
 class Place:
@@ -315,6 +360,101 @@
     ]
 
 
+class Overlap:
+    def __init__(self, place, copies, planes, grad, extended, buffers, final):
+        self.place, self.copies, self.planes, self.final = place, copies, planes, final
+        self.grad, self.extended = grad, extended
+        self.from_left, self.from_up, self.from_right, self.from_down, self.from_corner = buffers
+        count, tall, size = grad.shape[1:]
+        self.last, height = count - 1, tall - size
+        self.top, self.middle = pl.ds(0, size), pl.ds(size, height - size)
+        self.below, self.own = pl.ds(height, size), pl.ds(0, height)
+        self.block = [pl.ds(j * size, size) for j in range(self.last)]
+        self.ups, self.downs = {}, {}
+
+    def rows(self, j):
+        up, down = self.place.at(-1, 0), self.place.at(1, 0)
+        for p in self.planes:
+            self.ups[p, j] = self.copies.start(
+                self.grad.at[p, j, self.below], self.from_up.at[p, j], down
+            )
+            if not self.final:
+                self.downs[p, j] = self.copies.start(
+                    self.grad.at[p, j, self.top], self.from_down.at[p, j], up
+                )
+
+    def start(self):
+        right = self.place.at(0, 1)
+        self.sides = [
+            self.copies.start(self.grad.at[p, self.last], self.from_left.at[p], right)
+            for p in self.planes
+        ]
+        for j in range(1, self.last):
+            self.rows(j)
+
+    def first(self):
+        for p, side in zip(self.planes, self.sides):
+            side.wait_recv()
+            self.grad[p, 0] += self.from_left[p]
+        self.rows(0)
+        if not self.final:
+            left = self.place.at(0, -1)
+            self.middles = [
+                self.copies.start(self.grad.at[p, 0, self.middle], self.from_right.at[p], left)
+                for p in self.planes
+            ]
+
+    def corner(self):
+        left = self.place.at(0, -1)
+        self.corners = {}
+        for p in self.planes:
+            self.copies.sent(self.ups[p, 0])
+            self.copies.sent(self.downs[p, 0])
+            self.ups[p, 0].wait_recv()
+            self.grad[p, 0, self.top] += self.from_up[p, 0]
+            self.downs[p, 0].wait_recv()
+            self.grad[p, 0, self.below] += self.from_down[p, 0]
+            for k, lines in enumerate((self.top, self.below)):
+                self.corners[p, k] = self.copies.start(
+                    self.grad.at[p, 0, lines], self.from_corner.at[p, k], left
+                )
+
+    def update(self):
+        grad, extended, last = self.grad, self.extended, self.last
+        top, middle, below = self.top, self.middle, self.below
+        for p in self.planes:
+            extended[p % 2][p // 2, 0] -= STEP_OBJECT * grad[p, 0]
+        for j in range(1, last):
+            for p in self.planes:
+                self.ups[p, j].wait_recv()
+                self.downs[p, j].wait_recv()
+                extended[p % 2][p // 2, j, middle] -= STEP_OBJECT * grad[p, j, middle]
+                extended[p % 2][p // 2, j, top] -= STEP_OBJECT * (grad[p, j, top] + self.from_up[p, j])
+                extended[p % 2][p // 2, j, below] -= STEP_OBJECT * (grad[p, j, below] + self.from_down[p, j])
+        for p, copy in zip(self.planes, self.middles):
+            copy.wait_recv()
+            extended[p % 2][p // 2, last, middle] -= STEP_OBJECT * self.from_right[p]
+            for k, lines in enumerate((top, below)):
+                self.corners[p, k].wait_recv()
+                extended[p % 2][p // 2, last, lines] -= STEP_OBJECT * self.from_corner[p, k]
+
+    def keep(self, new_field):
+        for j in range(self.last):
+            for p in self.planes:
+                new_field[p, :, self.block[j]] = (
+                    self.extended[p % 2][p // 2, j, self.own] - STEP_OBJECT * self.grad[p, j, self.own]
+                )
+
+    def complete(self, new_field):
+        for j in list(range(1, self.last)) + [0]:
+            for p in self.planes:
+                self.ups[p, j].wait_recv()
+                new_field[p, self.top, self.block[j]] -= STEP_OBJECT * self.from_up[p, j]
+
+
+SLICE_PLANES = ((0, 2), (1, 3))
+
+
 def program_kernel(
     tiles,
     cols,
@@ -327,12 +467,17 @@
     table_hbm,
     new_field,
     new_probe,
-    extended,
+    object_first,
+    object_second,
     grad,
     beam,
     grad_beam,
     measured,
     table,
+    windows,
+    spread,
+    back,
+    patches,
     from_left,
     from_up,
     from_right,
@@ -342,20 +487,23 @@
 ):
     sums, (local_sem, send, recv) = rest[:-3], rest[-3:]
     sums = [sums[: len(sums) // 2], sums[len(sums) // 2 :]]
+    extended = (object_first, object_second)
     planes, count, tall, size = grad.shape
     last = count - 1
     height = tall - size
     slots = measured.shape[0]
     step_probe = 1.0 / (slots * tiles * cols)
-    top, middle, below = pl.ds(0, size), pl.ds(size, height - size), pl.ds(height, size)
-    own = pl.ds(0, height)
+    top, below, own = pl.ds(0, size), pl.ds(height, size), pl.ds(0, height)
     block = [pl.ds(j * size, size) for j in range(last)]
-    every = range(planes)
     place = Place(tiles, cols)
     copies = Copies(send, recv)
-    up, down, left, right = place.at(-1, 0), place.at(1, 0), place.at(0, -1), place.at(0, 1)
-
-    loads = [(field.at[:, :, block[j]], extended.at[:, j, own, :]) for j in range(last)]
+    up, left = place.at(-1, 0), place.at(0, -1)
+
+    loads = [
+        (field.at[p, :, block[j]], extended[p % 2].at[p // 2, j, own])
+        for p in range(planes)
+        for j in range(last)
+    ]
     loads += [(probe_hbm, beam), (table_hbm, table), (measured_hbm, measured)]
     loads = [
         pltpu.make_async_copy(source, target, local_sem.at[k])
@@ -365,97 +513,93 @@
         load.start()
     greet(met(place))
 
-    halos = {
-        (p, j): copies.start(field.at[p, top, block[j]], extended.at[p, j, below], up)
-        for j in range(last)
-        for p in every
-    }
-    sides = [
-        copies.start(field.at[p, :, block[0]], extended.at[p, last, own], left) for p in every
-    ]
-    corners = []
-    for p in every:
-        halos[p, 0].wait_recv()
-        corners.append(
-            copies.start(extended.at[p, 0, below], extended.at[p, last, below], left)
+    halos, sides, corners = {}, {}, {}
+
+    def send_halo(p, j):
+        halos[p, j] = copies.start(
+            field.at[p, top, block[j]], extended[p % 2].at[p // 2, j, below], up
         )
+
+    def pass_corners(which):
+        for p in SLICE_PLANES[which]:
+            halos[p, 0].wait_recv()
+            corners[p] = copies.start(
+                extended[p % 2].at[p // 2, 0, below], extended[p % 2].at[p // 2, last, below], left
+            )
+
+    def take_halo(which):
+        for p in SLICE_PLANES[which]:
+            for copy in [halos[p, j] for j in range(1, last)] + [sides[p], corners[p]]:
+                copy.wait_recv()
+
+    for which in SLICE_PLANES:
+        for p in which:
+            send_halo(p, 0)
+        for p in which:
+            sides[p] = copies.start(
+                field.at[p, :, block[0]], extended[p % 2].at[p // 2, last, own], left
+            )
+        for j in range(1, last):
+            for p in which:
+                send_halo(p, j)
+    pass_corners(0)
     for load in loads:
         load.wait()
-    for copy in list(halos.values())[planes:] + sides + corners:
-        copy.wait_recv()
-    copies.finish()
-
+    take_halo(0)
+
+    refs = (rows, columns, counts, measured, extended, beam, table, grad, grad_beam)
+    work = Positions(refs + (windows, spread, back, patches), size, slots)
+    waiting = None
     for sweep in range(ITERS):
-        add_gradients(
-            rows, columns, counts, measured, extended, beam, table, grad, grad_beam, slots
-        )
         final = sweep == ITERS - 1
+        landed = (from_left.at[sweep], from_up.at[sweep], from_right, from_down, from_corner)
+        zeroth, first = [
+            Overlap(place, copies, which, grad, extended, landed, final) for which in SLICE_PLANES
+        ]
+        for step in range(work.groups):
+            work.propagate(step)
+            if step == 0 and sweep == 0:
+                pass_corners(1)
+        if sweep == 0:
+            take_halo(1)
+        else:
+            waiting.update()
+        copies.finish()
+        work.clear(SLICE_PLANES[1])
+        lax.fori_loop(0, work.groups, lambda step, carry: (work.diffract(step), carry)[1], 0)
+        first.start()
+        for step in range(work.groups):
+            work.return_back(step)
+            if step == 0:
+                first.first()
         reduce = ProbeSum(place, copies, grad_beam, *sums[sweep])
         reduce.scatter_pair()
-        sides = [
-            copies.start(grad.at[p, last], from_left.at[sweep, p], right) for p in every
-        ]
-        ups, downs = {}, {}
-
-        def send_rows(p, j):
-            ups[p, j] = copies.start(grad.at[p, j, below], from_up.at[sweep, p, j], down)
-            if not final:
-                downs[p, j] = copies.start(grad.at[p, j, top], from_down.at[p, j], up)
-
-        for j in range(1, last):
-            for p in every:
-                send_rows(p, j)
-        reduce.scatter_tiles()
-        for p in every:
-            sides[p].wait_recv()
-            grad[p, 0] += from_left[sweep, p]
-            send_rows(p, 0)
+        for step in range(work.groups):
+            work.put_first(step)
+            if step == 0:
+                reduce.scatter_tiles()
+        zeroth.start()
         if final:
+            zeroth.first()
             reduce.sum_column()
-            for j in range(last):
-                for p in every:
-                    new_field[p, :, block[j]] = extended[p, j, own] - STEP_OBJECT * grad[p, j, own]
+            first.keep(new_field)
+            zeroth.keep(new_field)
             reduce.gather_tiles()
-            for j in list(range(1, last)) + [0]:
-                for p in every:
-                    ups[p, j].wait_recv()
-                    new_field[p, top, block[j]] -= STEP_OBJECT * from_up[sweep, p, j]
+            first.complete(new_field)
+            zeroth.complete(new_field)
             reduce.gather_pair()
             new_probe[...] = beam[...] - step_probe * reduce.result()
+            copies.finish()
         else:
-            middles = [
-                copies.start(grad.at[p, 0, middle], from_right.at[p], left) for p in every
-            ]
+            first.corner()
+            zeroth.first()
             reduce.sum_column()
             reduce.gather_tiles()
-            corners = {}
-            for p in every:
-                copies.sent(ups[p, 0])
-                copies.sent(downs[p, 0])
-                for way, landed, lines in ((ups, from_up.at[sweep], top), (downs, from_down, below)):
-                    way[p, 0].wait_recv()
-                    grad[p, 0, lines] += landed[p, 0]
-                for k, lines in enumerate((top, below)):
-                    corners[p, k] = copies.start(
-                        grad.at[p, 0, lines], from_corner.at[p, k], left
-                    )
-                extended[p, 0] -= STEP_OBJECT * grad[p, 0]
+            zeroth.corner()
             reduce.gather_pair()
-            for j in range(1, last):
-                for p in every:
-                    ups[p, j].wait_recv()
-                    downs[p, j].wait_recv()
-                    extended[p, j, middle] -= STEP_OBJECT * grad[p, j, middle]
-                    extended[p, j, top] -= STEP_OBJECT * (grad[p, j, top] + from_up[sweep, p, j])
-                    extended[p, j, below] -= STEP_OBJECT * (grad[p, j, below] + from_down[p, j])
-            for p in every:
-                middles[p].wait_recv()
-                extended[p, last, middle] -= STEP_OBJECT * from_right[p]
-                for k, lines in enumerate((top, below)):
-                    corners[p, k].wait_recv()
-                    extended[p, last, lines] -= STEP_OBJECT * from_corner[p, k]
+            zeroth.update()
             beam[...] -= step_probe * reduce.result()
-        copies.finish()
+            waiting = first
 
 
 def local(table, tiles, cols, object_field, probe, row_offsets, col_offsets, counts, measured):
@@ -477,12 +621,17 @@
         in_specs=[smem] * 3 + [hbm] * 4,
         out_specs=[vmem] * 2,
         scratch_shapes=[
-            pltpu.VMEM((planes, last + 1, tall, size), f32),
+            pltpu.VMEM((planes // 2, last + 1, tall, size), f32),
+            pltpu.VMEM((planes // 2, last + 1, tall, size), f32),
             pltpu.VMEM((planes, last + 1, tall, size), f32),
             pltpu.VMEM(flat, f32),
             pltpu.VMEM(flat, f32),
             pltpu.VMEM((slots, size, size), f32),
             pltpu.VMEM(table.shape, bf16),
+            pltpu.VMEM((slots, 2, size, size), f32),
+            pltpu.VMEM((slots, probe.shape[1], 2, size, size), f32),
+            pltpu.VMEM((slots, probe.shape[1], 2, size, size), f32),
+            pltpu.VMEM((slots, 2, size, size), f32),
             pltpu.VMEM((ITERS, planes, tall, size), f32),
             pltpu.VMEM((ITERS, planes, last, size, size), f32),
             pltpu.VMEM((planes, height - size, size), f32),
@@ -490,7 +639,7 @@
             pltpu.VMEM((planes, 2, size, size), f32),
             *ProbeSum.scratch(*flat, tiles, cols),
             *ProbeSum.scratch(*flat, tiles, cols),
-            pltpu.SemaphoreType.DMA((last + 3,)),
+            pltpu.SemaphoreType.DMA((planes * last + 3,)),
             pltpu.SemaphoreType.DMA((needed,)),
             pltpu.SemaphoreType.DMA((needed,)),
         ],

time: 118 us -> 115 us (0.975)
  Pallas kernels: 113 us -> 111 us
    pallas_call x1, Pallas kernels: 113 us -> 111 us  [local(): pl.pallas_call(functools.partial(program_kernel, tiles, cols), out_shape=...]
where the time goes in v3:
time: 115 us
  Pallas kernels  111 us (97%)
  local copies, waits for them, and re-layouts  3.14 us (3%)
  between operations  1.29 us (1%)
    pallas_call x1, Pallas kernels, local(): pl.pallas_call(functools.partial(program_kernel, tiles, cols), out_shape=...  111 us
    unnamed x4, local copies, waits for them, and re-layouts  3.14 us

profile of v3, /device:TPU:1, one launch (start us, length us, event | category | flops | bytes accessed | tf_op | source)
XLA Modules:
  0.0 115.3 jit_solution(8446921641140112389)
XLA Ops:
  1.3 110.9 %ptychography.1 = (f32[4,256,256]{2,1,0:T(8,128)}, f32[1024,128]{1,0:T(8,128)}) custom-call(s32[8]{0:T(128)} %bitcast.14, s32[8]{0:T(128)} %bitcast.15, s32[1]{0:T(128)} %bitcast.8.counts, f32[4,256,256]{2,1,0:T(8,128)} %bitcast.11, f32[1024,128]{1,0:T(8,128)} %bitcast.12, f32[8,128,128]{2,1,0:T(8,128)} %bitcast.13, bf16[8,256,256]{2,1,0:T(8,128)(2,1)} %constant.2.clone.table_hbm), custom_call_target="tpu_custom_call" | custom-call | flops 25769803776 | bytes 5242880 | tf_op jit(solution)/shard_map/ptychography/pallas_call | solution.py:618
  112.2 0.0 copy-start
  112.2 2.3 %copy.12 = f32[2,2,256,256]{3,2,1,0:T(8,128)} copy(f32[2,2,256,256]{3,2,1,0:T(8,128)} %bitcast.9) | data formatting | bytes 2097152
  114.5 0.0 copy-done
  114.5 0.8 copy.13
Async XLA Ops:
  112.2 2.4 %copy-start = (f32[1024,128]{1,0:T(8,128)S(1)}, f32[1024,128]{1,0:T(8,128)}, u32[]{:S(2)}) copy-start(f32[1024,128]{1,0:T(8,128)} %get-tuple-element.5) | copy-start | bytes 1572868

commit v4 on v3

--- a/solution.py
+++ b/solution.py
@@ -77,6 +77,7 @@
 
 
 GROUP = 4
+LINE = 4
 
 
 class Positions:
@@ -149,7 +150,8 @@
         for spot, o, backs in zip(spots, second, back):
             for m in self.modes:
                 self.back[spot[0], m, 0], self.back[spot[0], m, 1] = conj_times(o, backs[m])
-        self.put(spots, patches, (1, 3), False)
+        for spot, patch in zip(spots, patches):
+            self.patches[spot[0], 1], self.patches[spot[0], 3] = patch
 
     def return_back(self, step):
         spots, beams = self.spots(step), self.beams()
@@ -168,16 +170,12 @@
                     self.grad_beam[pl.ds(start, n)] += term
         for spot, backs in zip(spots, back):
             patch = total([conj_times(b, g) for b, g in zip(beams, backs)])
-            self.patches[spot[0], 0], self.patches[spot[0], 1] = patch
-
-    def put_first(self, step):
+            self.patches[spot[0], 0], self.patches[spot[0], 2] = patch
+
+    def place_patches(self, step, planes):
         spots = self.spots(step)
-        patches = [(self.patches[s[0], 0], self.patches[s[0], 1]) for s in spots]
-        self.put(spots, patches, (0, 2), step == 0)
-
-    def clear(self, planes):
-        for p in planes:
-            self.grad[p] = jnp.zeros(self.grad.shape[1:], f32)
+        patches = [[self.patches[s[0], p] for p in planes] for s in spots]
+        self.put(spots, patches, planes, step == 0)
 
     def put(self, spots, patches, planes, fresh):
         n = self.n
@@ -266,58 +264,67 @@
         self.place, self.copies = place, copies
         self.grad, self.pair, self.pieces, self.column, self.halves = grad, pair, pieces, column, halves
         self.half = grad.shape[0] // 2
-        self.piece = self.half // place.tiles
+        self.piece = self.half // (pieces.shape[0] + 1)
         self.core = lax.rem(place.c, 2)
         self.partner = (place.t, place.c + 1 - 2 * self.core)
         self.mine = pl.ds(self.core * self.half, self.half)
         self.others = pl.ds((1 - self.core) * self.half, self.half)
 
+    @staticmethod
+    def plane(place):
+        found = []
+        chips = place.cols // 2
+        for k in range(1, place.tiles // LINE * chips):
+            t, c = place.at(k // chips * LINE, 2 * (k % chips))
+            found.append((t // LINE * chips + c // 2, (t, c)))
+        return found
+
+    @staticmethod
+    def line(place):
+        start = place.t // LINE * LINE
+        return [(start + lax.rem(place.t + k, LINE), place.c) for k in range(1, LINE)]
+
+    def part(self, number):
+        return pl.ds(self.core * self.half + number * self.piece, self.piece)
+
+    def number(self):
+        return self.place.t // LINE * (self.place.cols // 2) + self.place.c // 2
+
     def scatter_pair(self):
         self.step = self.copies.start(self.grad.at[self.others], self.pair, self.partner)
 
-    def scatter_tiles(self):
+    def scatter_plane(self):
         self.step.wait_recv()
         self.grad[self.mine] += self.pair[...]
-        place, piece = self.place, self.piece
-        self.steps = []
-        for k in range(1, place.tiles):
-            peer = lax.rem(place.t + k, place.tiles)
-            source = self.grad.at[pl.ds(self.core * self.half + peer * piece, piece)]
-            self.steps.append(
-                self.copies.start(source, self.pieces.at[k - 1], (peer, place.c))
-            )
-
-    def sum_column(self):
-        place, piece = self.place, self.piece
-        value = self.grad[pl.ds(self.core * self.half + place.t * piece, piece)]
+        self.steps = [
+            self.copies.start(self.grad.at[self.part(number)], self.pieces.at[k], device)
+            for k, (number, device) in enumerate(self.plane(self.place))
+        ]
+
+    def sum_line(self):
+        value = self.grad[self.part(self.number())]
         for k, step in enumerate(self.steps):
             step.wait_recv()
             value += self.pieces[k]
-        chips = place.cols // 2
-        chip = place.c // 2
-        self.column[chip] = value
-        self.steps = []
-        for k in range(1, chips):
-            peer = (place.t, lax.rem(place.c + 2 * k, place.cols))
-            self.steps.append(
-                self.copies.start(self.column.at[chip], self.column.at[chip], peer)
-            )
-
-    def gather_tiles(self):
+        spot = lax.rem(self.place.t, LINE)
+        self.column[spot] = value
+        self.steps = [
+            self.copies.start(self.column.at[spot], self.column.at[spot], device)
+            for device in self.line(self.place)
+        ]
+
+    def gather_plane(self):
         for step in self.steps:
             step.wait_recv()
-        place, piece = self.place, self.piece
         value = self.column[0]
-        for k in range(1, place.cols // 2):
+        for k in range(1, LINE):
             value += self.column[k]
-        own = pl.ds(self.core * self.half + place.t * piece, piece)
+        own = self.part(self.number())
         self.halves[own] = value
-        self.steps = []
-        for k in range(1, place.tiles):
-            peer = lax.rem(place.t + k, place.tiles)
-            self.steps.append(
-                self.copies.start(self.halves.at[own], self.halves.at[own], (peer, place.c))
-            )
+        self.steps = [
+            self.copies.start(self.halves.at[own], self.halves.at[own], device)
+            for _, device in self.plane(self.place)
+        ]
 
     def gather_pair(self):
         for step in self.steps:
@@ -332,32 +339,24 @@
 
     @staticmethod
     def copies_needed(tiles, cols):
-        return 2 * tiles + cols // 2 - 1
+        return tiles * cols // (2 * LINE) * 2 + LINE - 1
 
     @staticmethod
     def scratch(rows, lanes, tiles, cols):
         half = rows // 2
-        piece = half // tiles
+        parts = tiles * cols // (2 * LINE)
+        piece = half // parts
         return [
             pltpu.VMEM((half, lanes), f32),
-            pltpu.VMEM((tiles - 1, piece, lanes), f32),
-            pltpu.VMEM((cols // 2, piece, lanes), f32),
+            pltpu.VMEM((parts - 1, piece, lanes), f32),
+            pltpu.VMEM((LINE, piece, lanes), f32),
             pltpu.VMEM((rows, lanes), f32),
         ]
 
 
 def met(place):
-    devices = [place.at(k, 0) for k in range(1, place.tiles)]
-    return devices + [
-        place.at(0, k) for k in range(1, place.cols) if k % 2 == 0 or k in (1, place.cols - 1)
-    ]
-
-
-def met(place):
-    devices = [place.at(k, 0) for k in range(1, place.tiles)]
-    return devices + [
-        place.at(0, k) for k in range(1, place.cols) if k % 2 == 0 or k in (1, place.cols - 1)
-    ]
+    sides = [place.at(*way) for way in ((-1, 0), (1, 0), (0, -1), (0, 1))]
+    return [device for _, device in ProbeSum.plane(place)] + ProbeSum.line(place) + sides
 
 
 class Overlap:
@@ -565,37 +564,35 @@
         else:
             waiting.update()
         copies.finish()
-        work.clear(SLICE_PLANES[1])
         lax.fori_loop(0, work.groups, lambda step, carry: (work.diffract(step), carry)[1], 0)
-        first.start()
         for step in range(work.groups):
             work.return_back(step)
-            if step == 0:
-                first.first()
         reduce = ProbeSum(place, copies, grad_beam, *sums[sweep])
         reduce.scatter_pair()
         for step in range(work.groups):
-            work.put_first(step)
+            work.place_patches(step, SLICE_PLANES[0])
             if step == 0:
-                reduce.scatter_tiles()
+                reduce.scatter_plane()
         zeroth.start()
+        for step in range(work.groups):
+            work.place_patches(step, SLICE_PLANES[1])
+        first.start()
+        zeroth.first()
+        reduce.sum_line()
+        first.first()
         if final:
-            zeroth.first()
-            reduce.sum_column()
             first.keep(new_field)
             zeroth.keep(new_field)
-            reduce.gather_tiles()
+            reduce.gather_plane()
+            zeroth.complete(new_field)
             first.complete(new_field)
-            zeroth.complete(new_field)
             reduce.gather_pair()
             new_probe[...] = beam[...] - step_probe * reduce.result()
             copies.finish()
         else:
+            reduce.gather_plane()
+            zeroth.corner()
             first.corner()
-            zeroth.first()
-            reduce.sum_column()
-            reduce.gather_tiles()
-            zeroth.corner()
             reduce.gather_pair()
             zeroth.update()
             beam[...] -= step_probe * reduce.result()
@@ -631,7 +628,7 @@
             pltpu.VMEM((slots, 2, size, size), f32),
             pltpu.VMEM((slots, probe.shape[1], 2, size, size), f32),
             pltpu.VMEM((slots, probe.shape[1], 2, size, size), f32),
-            pltpu.VMEM((slots, 2, size, size), f32),
+            pltpu.VMEM((slots, planes, size, size), f32),
             pltpu.VMEM((ITERS, planes, tall, size), f32),
             pltpu.VMEM((ITERS, planes, last, size, size), f32),
             pltpu.VMEM((planes, height - size, size), f32),

time: 115 us -> 114 us (level)
  Pallas kernels: 111 us -> 109 us
    pallas_call x1, Pallas kernels: 111 us -> 109 us  [local(): pl.pallas_call(functools.partial(program_kernel, tiles, cols), out_shape=...]
where the time goes in v4:
time: 114 us; the launch traced here: 113 us
  Pallas kernels  109 us (96%)
  local copies, waits for them, and re-layouts  3.14 us (3%)
  between operations  1.29 us (1%)
    pallas_call x1, Pallas kernels, local(): pl.pallas_call(functools.partial(program_kernel, tiles, cols), out_shape=...  109 us
    unnamed x4, local copies, waits for them, and re-layouts  3.14 us

profile of v4, /device:TPU:1, one launch (start us, length us, event | category | flops | bytes accessed | tf_op | source)
XLA Modules:
  0.0 113.5 jit_solution(5079801417744178811)
XLA Ops:
  1.3 109.0 %ptychography.1 = (f32[4,256,256]{2,1,0:T(8,128)}, f32[1024,128]{1,0:T(8,128)}) custom-call(s32[8]{0:T(128)} %bitcast.14, s32[8]{0:T(128)} %bitcast.15, s32[1]{0:T(128)} %bitcast.8.counts, f32[4,256,256]{2,1,0:T(8,128)} %bitcast.11, f32[1024,128]{1,0:T(8,128)} %bitcast.12, f32[8,128,128]{2,1,0:T(8,128)} %bitcast.13, bf16[8,256,256]{2,1,0:T(8,128)(2,1)} %constant.2.clone.table_hbm), custom_call_target="tpu_custom_call" | custom-call | flops 25769803776 | bytes 5242880 | tf_op jit(solution)/shard_map/ptychography/pallas_call | solution.py:615
  110.3 0.0 copy-start
  110.3 2.3 %copy.12 = f32[2,2,256,256]{3,2,1,0:T(8,128)} copy(f32[2,2,256,256]{3,2,1,0:T(8,128)} %bitcast.9) | data formatting | bytes 2097152
  112.7 0.0 copy-done
  112.7 0.8 copy.13
Async XLA Ops:
  110.3 2.4 %copy-start = (f32[1024,128]{1,0:T(8,128)S(1)}, f32[1024,128]{1,0:T(8,128)}, u32[]{:S(2)}) copy-start(f32[1024,128]{1,0:T(8,128)} %get-tuple-element.5) | copy-start | bytes 1572868

commit v5 on v4

--- a/solution.py
+++ b/solution.py
@@ -384,24 +384,42 @@
 
     def start(self):
         right = self.place.at(0, 1)
-        self.sides = [
-            self.copies.start(self.grad.at[p, self.last], self.from_left.at[p], right)
+        self.edges = {
+            (p, k): self.copies.start(
+                self.grad.at[p, self.last, lines], self.from_left.at[p, lines], right
+            )
             for p in self.planes
-        ]
+            for k, lines in enumerate((self.top, self.below))
+        }
         for j in range(1, self.last):
             self.rows(j)
 
+    def start_inner(self):
+        right = self.place.at(0, 1)
+        self.sides = [
+            self.copies.start(
+                self.grad.at[p, self.last, self.middle], self.from_left.at[p, self.middle], right
+            )
+            for p in self.planes
+        ]
+
     def first(self):
+        for p in self.planes:
+            for k, lines in enumerate((self.top, self.below)):
+                self.edges[p, k].wait_recv()
+                self.grad[p, 0, lines] += self.from_left[p, lines]
+        self.rows(0)
+
+    def inner(self):
+        left = self.place.at(0, -1)
+        self.middles = []
         for p, side in zip(self.planes, self.sides):
             side.wait_recv()
-            self.grad[p, 0] += self.from_left[p]
-        self.rows(0)
-        if not self.final:
-            left = self.place.at(0, -1)
-            self.middles = [
-                self.copies.start(self.grad.at[p, 0, self.middle], self.from_right.at[p], left)
-                for p in self.planes
-            ]
+            self.grad[p, 0, self.middle] += self.from_left[p, self.middle]
+            if not self.final:
+                self.middles.append(
+                    self.copies.start(self.grad.at[p, 0, self.middle], self.from_right.at[p], left)
+                )
 
     def corner(self):
         left = self.place.at(0, -1)
@@ -577,23 +595,27 @@
         for step in range(work.groups):
             work.place_patches(step, SLICE_PLANES[1])
         first.start()
+        zeroth.start_inner()
+        first.start_inner()
+        reduce.sum_line()
         zeroth.first()
-        reduce.sum_line()
+        reduce.gather_plane()
         first.first()
+        zeroth.inner()
         if final:
+            first.inner()
+            zeroth.keep(new_field)
             first.keep(new_field)
-            zeroth.keep(new_field)
-            reduce.gather_plane()
             zeroth.complete(new_field)
+            reduce.gather_pair()
             first.complete(new_field)
-            reduce.gather_pair()
             new_probe[...] = beam[...] - step_probe * reduce.result()
             copies.finish()
         else:
-            reduce.gather_plane()
             zeroth.corner()
+            first.inner()
+            reduce.gather_pair()
             first.corner()
-            reduce.gather_pair()
             zeroth.update()
             beam[...] -= step_probe * reduce.result()
             waiting = first
@@ -607,7 +629,7 @@
     flat = (probe.shape[0] * probe.shape[1] * size, size)
     planes, last, tall = 4, width // size, height + size
     needed = planes * (2 * last + 2) + ITERS * ProbeSum.copies_needed(tiles, cols)
-    needed += planes * (1 + 2 * last + 1 + 2) + planes * (1 + last)
+    needed += planes * (3 + 2 * last + 1 + 2) + planes * (3 + last)
     work = ITERS * slots * probe.shape[1] * 8 * 3 * 2 * 256 * 256 * 128
     smem = pl.BlockSpec(memory_space=pltpu.SMEM)
     hbm = pl.BlockSpec(memory_space=pl.ANY)

time: 114 us -> 113 us (level)
  no operation moved by 1% of the time
where the time goes in v5:
time: 113 us
  Pallas kernels  108 us (96%)
  local copies, waits for them, and re-layouts  3.14 us (3%)
  between operations  1.29 us (1%)
    pallas_call x1, Pallas kernels, local(): pl.pallas_call(functools.partial(program_kernel, tiles, cols), out_shape=...  108 us
    unnamed x4, local copies, waits for them, and re-layouts  3.14 us

profile of v5, /device:TPU:1, one launch (start us, length us, event | category | flops | bytes accessed | tf_op | source)
XLA Modules:
  0.0 112.6 jit_solution(102406580643495858)
XLA Ops:
  1.3 108.1 %ptychography.1 = (f32[4,256,256]{2,1,0:T(8,128)}, f32[1024,128]{1,0:T(8,128)}) custom-call(s32[8]{0:T(128)} %bitcast.14, s32[8]{0:T(128)} %bitcast.15, s32[1]{0:T(128)} %bitcast.8.counts, f32[4,256,256]{2,1,0:T(8,128)} %bitcast.11, f32[1024,128]{1,0:T(8,128)} %bitcast.12, f32[8,128,128]{2,1,0:T(8,128)} %bitcast.13, bf16[8,256,256]{2,1,0:T(8,128)(2,1)} %constant.2.clone.table_hbm), custom_call_target="tpu_custom_call" | custom-call | flops 25769803776 | bytes 5242880 | tf_op jit(solution)/shard_map/ptychography/pallas_call | solution.py:637
  109.4 0.0 copy-start
  109.4 2.3 %copy.12 = f32[2,2,256,256]{3,2,1,0:T(8,128)} copy(f32[2,2,256,256]{3,2,1,0:T(8,128)} %bitcast.9) | data formatting | bytes 2097152
  111.8 0.0 copy-done
  111.8 0.8 copy.13
Async XLA Ops:
  109.4 2.4 %copy-start = (f32[1024,128]{1,0:T(8,128)S(1)}, f32[1024,128]{1,0:T(8,128)}, u32[]{:S(2)}) copy-start(f32[1024,128]{1,0:T(8,128)} %get-tuple-element.5) | copy-start | bytes 1572868
